TPU v7x, 128 devices: a whole 4x4x4 slice. The times are simulated.
128 devices in a mesh: ctx: 32 (over z_lo, x, y), fsdp: 4 (over z_hi, core).
Axes of the slice: x: 4, y: 4, z: 4 (z_hi: 2, z_lo: 2; z = z_hi * 2 + z_lo), core: 2. Of those that a mesh axis runs over, the one named last changes fastest.
Arguments:
- inputs: bfloat16 [4, 4096, 1024], P('fsdp', 'ctx'), may hold values from -6 to 6
- cotangent: bfloat16 [4, 4096, 1024], P('fsdp', 'ctx'), may hold values from -6 to 6
- qkv_weight: bfloat16 [1024, 2048], P('fsdp'), may hold values from -0.1875 to 0.1875
- out_weight: bfloat16 [1024, 1024], P('fsdp'), may hold values from -1 to 1
- gate_weight: bfloat16 [1024, 4608], P('fsdp'), may hold values from -0.1875 to 0.1875
- up_weight: bfloat16 [1024, 4608], P('fsdp'), may hold values from -0.1875 to 0.1875
- down_weight: bfloat16 [4608, 1024], P('fsdp'), may hold values from -0.09375 to 0.09375
- gain_attn: float32 [1024], replicated, may hold values from 0.5 to 1.5
- gain_query: float32 [64], replicated, may hold values from 0.1 to 1.9
- gain_key: float32 [64], replicated, may hold values from 0.1 to 1.9
- gain_ffn: float32 [1024], replicated, may hold values from 0.5 to 1.5
- block_order: int32 [64], replicated, may hold values from 0 to 63, each once
- doc_starts: int32 [4, 4], P('fsdp'), may hold values from 0 to 4095, as said below
Outputs:
- outputs: bfloat16 [4, 4096, 1024], P('fsdp', 'ctx')
- grad_inputs: bfloat16 [4, 4096, 1024], P('fsdp', 'ctx')
- grad_qkv_weight: float32 [1024, 2048], P('fsdp')
- grad_out_weight: float32 [1024, 1024], P('fsdp')
- grad_gate_weight: float32 [1024, 4608], P('fsdp')
- grad_up_weight: float32 [1024, 4608], P('fsdp')
- grad_down_weight: float32 [4608, 1024], P('fsdp')
- grad_gain_attn: float32 [1024], replicated
- grad_gain_query: float32 [64], replicated
- grad_gain_key: float32 [64], replicated
- grad_gain_ffn: float32 [1024], replicated
Inputs may be any that keep to these rules, and one draw needn't show every extreme that they name: `doc_starts`: for each sequence, 4 strictly increasing document starts: the first is 0, the last is 4095, all others lie at or after 4096 - 4096 // 4.
All inputs are finite; a program needn't handle non-finite values.
Results may differ from a plain program's by a relative error of at most 0.03.
Values may be sent and summed in bfloat16 or wider, within the bound.
A program may use at most 256 MiB of HBM per device.

v0:
```python
import functools
import math

import jax
import jax.numpy as jnp
from jax import lax
from jax.experimental import pallas as pl
from jax.experimental.pallas import tpu as pltpu
from jax.sharding import PartitionSpec as P

QUERY_HEADS = 16
KEY_VALUE_HEADS = 8
HEAD_SIZE = 64
FF = 4608
D = 1024
TOKENS = 128
RING = 32
QUARTER = 8
SLICE = 1152
HALF_FF = FF // 2
KEY_TILE = 1024
KEY_TILE_BACK = 1024
SEQ = 4096

EPSILON = 1e-05
ROPE_BASE = 1000000.0
SCORE_TO_EXP2 = float(HEAD_SIZE) ** (-0.5) * math.log2(math.e)

MESH = pl.DeviceIdType.MESH
ANY = pl.BlockSpec(memory_space=pl.ANY)
VMEM = pl.BlockSpec(memory_space=pltpu.VMEM)
SMEM = pl.BlockSpec(memory_space=pltpu.SMEM)
BF16 = jnp.bfloat16
F32 = jnp.float32
MIB = 1 << 20
STEPS = (1, 3, 2)


class Place:
    def __init__(self):
        self.ctx, self.fsdp = (lax.axis_index("ctx"), lax.axis_index("fsdp"))
        self.zl, self.x, self.y = (self.ctx // 16, (self.ctx // 4) % 4, self.ctx % 4)
        self.zh, self.core = (self.fsdp // 2, self.fsdp % 2)
        self.z = self.zh * 2 + self.zl

    def device(self, x=None, y=None, z=None, core=None):
        x = self.x if x is None else x
        y = self.y if y is None else y
        z = self.z if z is None else z
        core = self.core if core is None else core
        return ((z % 2) * 16 + x * 4 + y, (z // 2) * 2 + core)

    def sibling(self):
        return self.device(core=1 - self.core)

    def along(self, axis, step):
        coordinate = (getattr(self, axis) + step) % 4
        return coordinate, self.device(**{axis: coordinate})


class Wires:
    def __init__(self, sends, receives, locals_=None):
        self.sends, self.receives, self.locals_ = (sends, receives, locals_)
        self.pushed, self.moved = ([], 0)

    def push(self, source, target, device):
        at = len(self.pushed)
        copy = pltpu.make_async_remote_copy(
            src_ref=source,
            dst_ref=target,
            send_sem=self.sends.at[at],
            recv_sem=self.receives.at[at],
            device_id=device,
            device_id_type=MESH,
        )
        copy.start()
        self.pushed.append(copy)
        return copy

    def move(self, source, target):
        copy = pltpu.make_async_copy(source, target, self.locals_.at[self.moved])
        copy.start()
        self.moved += 1
        return copy

    def finish_sends(self):
        for copy in self.pushed:
            copy.wait_send()


def arrive(copies):
    for copy in copies:
        copy.wait_recv()


def greet(devices):
    barrier = pltpu.get_barrier_semaphore()
    for device in devices:
        pl.semaphore_signal(barrier, inc=1, device_id=device, device_id_type=MESH)
    pl.semaphore_wait(barrier, len(devices))


def wired_call(kernel, outs, ins, collective_id, name, copies, moves, scratch=(), in_specs=None,
               out_specs=None, vmem=32 * MIB, aliases=None):
    return pl.pallas_call(
        kernel,
        out_shape=outs,
        in_specs=[ANY] * len(ins) if in_specs is None else in_specs,
        out_specs=[ANY] * len(outs) if out_specs is None else out_specs,
        scratch_shapes=[
            *scratch,
            pltpu.SemaphoreType.DMA((copies,)),
            pltpu.SemaphoreType.DMA((copies,)),
            pltpu.SemaphoreType.DMA((max(moves, 1),)),
        ],
        compiler_params=pltpu.CompilerParams(
            collective_id=collective_id, has_side_effects=True, vmem_limit_bytes=vmem
        ),
        name=name,
        input_output_aliases=aliases or {},
    )(*ins)


def shape(*dims, dtype=BF16):
    return jax.ShapeDtypeStruct(dims, dtype)


class Pieces:
    def view(self, ref, at, skip=0):
        lead = [slice(None) if i is None else i for i in self.order(at)[skip:]]
        return ref.at[(*lead, *self.tail(at))]

    def open_dims(self, at):
        return tuple(n for n, i in zip(self.lead, self.order(at)) if i is None)

    def tail(self, at):
        first, width = self.columns(at)
        if not isinstance(first, int):
            first = pl.multiple_of(first, 128)
        return (slice(None), pl.ds(first, width))

    def tail_dims(self, at):
        return (self.rows, self.columns(at)[1])


def halved(first, width, at):
    if "half" not in at:
        return first, width
    return first + at["half"] * (width // 2), width // 2


class RowsByShard(Pieces):
    lead, rows = ((2, 2, 4, 4), 16)

    def __init__(self, width):
        self.width = width

    def order(self, at):
        return [at.get("zh"), at.get("zl"), at.get("x"), at.get("y")]

    def columns(self, at):
        return halved(0, self.width, at)


class RowsByPlane(Pieces):
    lead, rows = ((2, 4, 4), 16)

    def __init__(self, first, width):
        self.first, self.width = (first, width)

    def order(self, at):
        return [at.get("zh"), at.get("x"), at.get("y")]

    def columns(self, at):
        if "zl" not in at:
            return halved(self.first, self.width, at)
        half = self.width // 2
        return halved(self.first + half * at["zl"], half, at)


class ColumnsByY(Pieces):
    lead = (2, 4, 2)

    def __init__(self, rows):
        self.rows = rows

    def order(self, at):
        return [at.get("zh"), at.get("x"), at.get("zl")]

    def columns(self, at):
        return halved(at["y"] * 256, 256, at) if "y" in at else halved(0, D, at)


class ShardsByCore(Pieces):
    lead, rows = ((2, 2, 4, 4), 16)

    def __init__(self, width):
        self.width = width

    def order(self, at):
        return [at.get("zh"), at.get("half"), at.get("x"), at.get("y")]

    def columns(self, at):
        half = self.width // 2
        return (half * at["zl"], half) if "zl" in at else (0, self.width)


class OneCore(RowsByPlane):
    lead = (2, 2, 4, 4)

    def __init__(self, first, width, core):
        super().__init__(first, width)
        self.core = core

    def order(self, at):
        return [at.get("zh"), self.core, at.get("x"), at.get("y")]


def fix(at, axis, coordinate):
    if axis == "z":
        return {**at, "zh": coordinate // 2, "zl": coordinate % 2}
    return {**at, axis: coordinate}


def without(at, axis):
    return {a: i for a, i in at.items() if a != ("zl" if axis == "z" else axis)}


def in_turn(tasks):
    while tasks:
        tasks = [task for task in tasks if next(task, "over") != "over"]


def spread(here, wires, kind, ref, at, order, skip=0, direct=""):
    for axis in order:
        piece = kind.view(ref, at, skip)
        if axis == "z":
            copies = [wires.push(piece, piece, here.device(z=here.zh * 2 + 1 - here.zl))]
            yield
            arrive(copies)
        elif axis in direct:
            copies = [wires.push(piece, piece, here.along(axis, s)[1]) for s in STEPS]
            yield
            arrive(copies)
        else:
            (_, right), (_, left) = (here.along(axis, 1), here.along(axis, 3))
            from_left = wires.push(piece, piece, right)
            from_right = wires.push(piece, piece, left)
            yield
            relays = []
            for half, copy, step, onward in ((0, from_left, 3, right), (1, from_right, 1, left)):
                arrive([copy])
                passing = fix(at, axis, here.along(axis, step)[0])
                passing = kind.view(ref, {**passing, "half": half}, skip)
                relays.append(wires.push(passing, passing, onward))
            yield
            arrive(relays)
        at = without(at, axis)


def greet_rings(here, others=()):
    rings = [here.along(a, s)[1] for a in ("x", "y", "z") for s in STEPS]
    greet([*rings, here.sibling(), *others])


class Fetch:
    def __init__(self, here, wires):
        self.here, self.wires = (here, wires)
        self.zh, self.core, self.x, self.y = (here.zh, here.core, here.x, here.y)
        self.there = 1 - here.zl
        self.cross = [here.device(z=3 - here.z, core=(here.core + t) % 2) for t in range(2)]
        self.sibling = here.sibling()
        self.held = {"zh": 1 - here.zh, "zl": here.zl, "x": here.x, "y": here.y}

    def part(self, width):
        return pl.ds(pl.multiple_of(self.there * width, 128), width)

    def ff_columns(self, r, c):
        return pl.ds(pl.multiple_of(r * HALF_FF + c * SLICE, 128), SLICE)

    def rest(self, kind, whole, crossed, order, direct):
        yield
        arrive(crossed)
        yield from spread(
            self.here, self.wires, kind, whole, self.held, order, direct=direct
        )

    def narrow(self, shard, whole, first, width, order):
        columns = pl.ds(first, width)
        source = shard.at[self.x, self.y, :, columns]
        target = whole.at[self.zh, self.core, self.x, self.y, :, columns]
        crossed = [self.wires.push(source, target, self.cross[0])]
        yield
        arrive(crossed)
        held = without(self.held, "z")
        kind = OneCore(first, width, self.core)
        yield from spread(self.here, self.wires, kind, whole, held, order, direct="xy")
        passed = whole.at[1 - self.zh, self.core, :, :, :, columns]
        beside = [self.wires.push(passed, passed, self.sibling)]
        yield
        arrive(beside)

    def wide(self, shard, whole, order):
        crossed = [
            self.wires.push(
                shard.at[self.x, self.y, :, self.ff_columns(self.there, (self.core + t) % 2)],
                whole.at[self.zh, self.core, self.x, self.y, :, self.part(SLICE)],
                self.cross[t],
            )
            for t in range(2)
        ]
        yield from self.rest(ShardsByCore(HALF_FF), whole, crossed, order, "y")

    def down(self, shard, whole, order):
        columns = pl.ds(pl.multiple_of(self.y * 256, 256), 256)
        source = shard.at[self.x, self.there, :, columns]
        target = whole.at[self.zh, self.x, self.there, :, columns]
        crossed = [self.wires.push(source, target, self.cross[0])]
        yield from self.rest(ColumnsByY(144), whole, crossed, order, "x")

    def from_this_chip(self, narrow=(), wide=(), down=()):
        beside, kept = ([], [])
        for shard, whole in narrow:
            target = whole.at[self.zh, self.core]
            beside.append(self.wires.push(shard, target, self.sibling))
            kept.append(self.wires.move(shard, target))
        for shard, whole in wide:
            for r in range(2):
                target = whole.at[self.zh, self.core, :, :, :, pl.ds(r * SLICE, SLICE)]
                theirs = shard.at[:, :, :, self.ff_columns(r, 1 - self.core)]
                mine = shard.at[:, :, :, self.ff_columns(r, self.core)]
                beside.append(self.wires.push(theirs, target, self.sibling))
                kept.append(self.wires.move(mine, target))
        for shard, whole in down:
            kept.append(self.wires.move(shard, whole.at[self.zh]))
        for _ in range(6):
            yield
        arrive(beside)
        for copy in kept:
            copy.wait()


WIDE_FETCH = (
    (ShardsByCore(HALF_FF), ("y", "x", "z")),
    (ShardsByCore(HALF_FF), ("z", "y", "x")),
    (ColumnsByY(144), ("x", "z", "y")),
)


def gather_kernel(
    qkv, out, gate, up, down, qkv_all, out_all, gate_all, up_all, down_all, sends, receives, moves
):
    wires = Wires(sends, receives, moves)
    here = Place()
    fetch = Fetch(here, wires)
    greet_rings(here, fetch.cross)
    in_turn(
        [
            fetch.narrow(qkv, qkv_all, 0, 1024, ("x", "y")),
            fetch.narrow(qkv, qkv_all, 1024, 1024, ("y", "x")),
            fetch.narrow(out, out_all, 0, D, ("x", "y")),
            fetch.wide(gate, gate_all, WIDE_FETCH[0][1][:2]),
            fetch.wide(up, up_all, WIDE_FETCH[1][1][:2]),
            fetch.down(down, down_all, WIDE_FETCH[2][1][:2]),
            fetch.from_this_chip(
                ((qkv, qkv_all), (out, out_all)),
                ((gate, gate_all), (up, up_all)),
                ((down, down_all),),
            ),
        ]
    )
    wires.finish_sends()


def gather(qkv, out, gate, up, down):
    rows = (4, 4, 16)
    qkv, out, *wide = wired_call(
        gather_kernel,
        [
            shape(2, 2, *rows, 2048),
            shape(2, 2, *rows, D),
            shape(2, 2, *rows, HALF_FF),
            shape(2, 2, *rows, HALF_FF),
            shape(2, 4, 2, 144, D),
        ],
        (
            qkv.reshape(*rows, 2048),
            out.reshape(*rows, D),
            gate.reshape(*rows, FF),
            up.reshape(*rows, FF),
            down.reshape(4, 2, 144, D),
        ),
        1,
        "gather",
        3 * 8 + 9 + 6 + 5 + 6,
        7,
    )
    return qkv.reshape(D, 2048), out.reshape(D, D), wide


def fetch_last(here, wires, wide):
    for (kind, order), whole in zip(WIDE_FETCH, wide):
        at = {"zh": 1 - here.zh, "zl": here.zl, "x": here.x, "y": here.y}
        for axis in order[:2]:
            at = without(at, axis)
        yield spread(here, wires, kind, whole, at, order[2:])


WIDE = (
    (0, RowsByShard(HALF_FF), ("z", "x", "y"), ("y", "x", "z")),
    (1, RowsByShard(HALF_FF), ("x", "y", "z"), ("z", "y", "x")),
    (2, ColumnsByY(144), ("y", "z", "x"), ("x", "z", "y")),
    (3, ColumnsByY(32), ("y", "z", "x"), ("x", "z", "y")),
)
NARROW = (
    (0, RowsByPlane(0, 1024), ("z", "x", "y"), ("z", "y", "x")),
    (0, RowsByPlane(1024, 1024), ("x", "y", "z"), ("x", "z", "y")),
)
FIRST_DIRECT = ("y", "y", "x", "x")
WIDE_DIMS = (
    (2, 2, 4, 4, 16, HALF_FF),
    (2, 2, 4, 4, 16, HALF_FF),
    (2, 4, 2, 144, D),
    (2, 4, 2, 32, D),
)
QKV_DIMS = (2, 4, 4, 16, 2048)
PIECE_DIMS = ((16, HALF_FF), (16, HALF_FF), (144, 256), (32, 256))


def slot_shapes(parts):
    found = []
    for _, kind, order, _ in parts:
        at = {}
        for axis in order:
            at = fix(at, axis, 0)
            found.append((6, *kind.open_dims(at), *kind.tail_dims({**at, "half": 0})))
    return found


def each_block(kind, at, body):
    dims = kind.open_dims(at)

    def step(i, _):
        inner, rest = ([], i)
        for n in reversed(dims):
            inner.insert(0, rest % n)
            rest = rest // n
        picks = iter(inner)
        lead = [next(picks) if o is None else o for o in kind.order(at)]
        body((*lead, *kind.tail(at)), (*inner, slice(None), slice(None)))
        return 0

    lax.fori_loop(0, math.prod(dims), step, 0)


def reduce_one(here, wires, kind, grad, total, slots, order, direct_from):
    at = {}
    for step, axis in enumerate(order):
        source, slot = (grad if step == 0 else total, slots[step])
        (right_place, right), (left_place, left) = (here.along(axis, 1), here.along(axis, 3))
        far_place, _ = here.along(axis, 2)
        mine = fix(at, axis, getattr(here, axis))

        def half_of(place, half):
            return {**fix(at, axis, place), "half": half}

        if step >= direct_from:
            copies = [
                wires.push(
                    kind.view(source, half_of(here.along(axis, s)[0], half)),
                    slot.at[2 * j + half],
                    here.along(axis, s)[1],
                )
                for j, s in enumerate(STEPS)
                for half in range(2)
            ]
            yield
            arrive(copies)
            for half in range(2):

                def add_all(whole, part):
                    value = total[whole].astype(F32)
                    for j in range(3):
                        value += slot[(2 * j + half, *part)].astype(F32)
                    total[whole] = value.astype(BF16)

                each_block(kind, {**mine, "half": half}, add_all)
            at = mine
            continue
        relays = [
            wires.push(kind.view(source, half_of(far_place, 0)), slot.at[4], right),
            wires.push(kind.view(source, half_of(far_place, 1)), slot.at[5], left),
        ]
        arriving = [
            wires.push(kind.view(source, half_of(right_place, 1)), slot.at[1], right),
            wires.push(kind.view(source, half_of(left_place, 0)), slot.at[2], left),
        ]
        kept = []
        if step == 0:
            for where in (half_of(right_place, 0), half_of(left_place, 1), mine):
                kept.append(wires.move(kind.view(source, where), kind.view(total, where)))
        yield
        for j, place, half, target, onward in (
            (4, right_place, 0, 0, right),
            (5, left_place, 1, 3, left),
        ):
            if kept:
                kept.pop(0).wait()
            arrive([relays[j - 4]])

            def pass_on(whole, part):
                value = slot[(j, *part)].astype(F32) + total[whole].astype(F32)
                slot[(j, *part)] = value.astype(BF16)

            each_block(kind, half_of(place, half), pass_on)
            arriving.append(wires.push(slot.at[j], slot.at[target], onward))
        yield
        if kept:
            kept.pop(0).wait()
        arrive(arriving)
        for half in range(2):

            def add_up(whole, part):
                value = total[whole].astype(F32) + slot[(half, *part)].astype(F32)
                total[whole] = (value + slot[(2 + half, *part)].astype(F32)).astype(BF16)

            each_block(kind, {**mine, "half": half}, add_up)
        at = mine


def reduce_weights_kernel(*refs):
    grad, gains = refs[4:6]
    nears, (gate_beside, up_beside, qkv_out, gains_out) = (refs[6:10], refs[10:14])
    total, slots = (refs[14], refs[15:21])
    gain_slots, sends, receives, moves = refs[21:]
    besides = (gate_beside, up_beside)

    here = Place()
    wires = Wires(sends, receives, moves)
    core = here.core
    sibling = here.sibling()
    greet_rings(here)
    held = {"zh": here.zh, "zl": here.zl, "x": here.x, "y": here.y}

    def all_gains():
        sums = gains[...]
        for stage, axis in enumerate(("core", "x", "y", "z")):
            me = getattr(here, axis)
            gain_slots[stage, me] = sums
            source = gain_slots.at[stage, me]
            if axis == "core":
                others = [sibling]
            else:
                others = [here.along(axis, s)[1] for s in STEPS]
            copies = [wires.push(source, source, device) for device in others]
            yield
            arrive(copies)
            sums = gain_slots[stage, 0] + gain_slots[stage, 1]
            if axis != "core":
                sums = sums + gain_slots[stage, 2] + gain_slots[stage, 3]
        gains_out[...] = sums

    def narrow(p):
        _, kind, order, back = NARROW[p]
        yield from reduce_one(
            here, wires, kind, grad, total, slots[3 * p : 3 * p + 3], order, 1
        )
        own = wires.move(kind.view(total, held), kind.view(qkv_out, held, 1))
        own.wait()
        yield from spread(here, wires, kind, qkv_out, held, back, 1, direct="xy")

    def wide(p):
        _, kind, _, back = WIDE[p]
        at = held
        for axis in back[:2]:
            at = without(at, axis)
        yield from spread(here, wires, kind, nears[p], at, back[2:], 1)
        if p < 2:
            copies = [wires.push(nears[p].at[1 - core], besides[p], sibling)]
            yield
            arrive(copies)

    in_turn([narrow(p) for p in range(2)] + [wide(p) for p in range(4)] + [all_gains()])
    wires.finish_sends()


def reduce_weights(nears, qkv, gains):
    outs = [
        *(shape(*d[1:]) for d in WIDE_DIMS),
        shape(*WIDE_DIMS[0][2:]),
        shape(*WIDE_DIMS[1][2:]),
        shape(*QKV_DIMS[1:]),
        shape(*gains.shape, dtype=F32),
    ]
    scratch = [pltpu.VMEM(QKV_DIMS, BF16)]
    scratch += [pltpu.VMEM(s, BF16) for s in slot_shapes(NARROW)]
    scratch += [pltpu.VMEM((4, 4, *gains.shape), F32)]
    gate, up, down, out, gate_beside, up_beside, qkv, gains = wired_call(
        reduce_weights_kernel,
        outs,
        [*nears, qkv.reshape(QKV_DIMS), gains],
        2,
        "reduce_weights",
        10 + 2 * (18 + 7) + 1 + 3 * 4 + 2,
        2 * 4,
        scratch,
        [ANY] * 5 + [VMEM],
        [ANY] * 7 + [VMEM],
        vmem=40 * MIB,
        aliases={i: i for i in range(4)},
    )
    core = lax.axis_index("fsdp") % 2

    def joined(near, beside):
        own = lax.dynamic_index_in_dim(near, core, 0, keepdims=False).reshape(256, HALF_FF)
        beside = beside.reshape(256, HALF_FF)
        first, second = (jnp.where(core == 0, own, beside), jnp.where(core == 0, beside, own))
        pieces = [f[:, r * SLICE : (r + 1) * SLICE] for r in range(2) for f in (first, second)]
        return jnp.concatenate(pieces, axis=1)

    gate, up = (joined(gate, gate_beside), joined(up, up_beside))
    return (
        qkv.reshape(256, 2048),
        out.reshape(256, D),
        gate,
        up,
        down.reshape(SLICE, D),
        gains,
    )


def head_columns(head):
    return pl.ds(pl.multiple_of(head * 128, 128), 128)


def seats(here):
    me = here.ctx
    quarter, seat = (me // QUARTER, me % QUARTER)
    near = [quarter * QUARTER + (seat + s) % QUARTER for s in range(1, QUARTER)]
    far = [(me + s) % RING for s in range(1, RING)]
    return me, seat, near, far


def to_heads_kernel(query, key_value, query_out, key_value_out, sends, receives, moves):
    here = Place()
    wires = Wires(sends, receives, moves)
    me, seat, near, far = seats(here)
    greet([(k, here.fsdp) for k in far])
    copies = [
        wires.push(query.at[:, head_columns(k % QUARTER)], query_out.at[seat], (k, here.fsdp))
        for k in near
    ]
    copies += [
        wires.push(key_value.at[:, head_columns(k % QUARTER)], key_value_out.at[me], (k, here.fsdp))
        for k in far
    ]
    kept = [
        wires.move(query.at[:, head_columns(seat)], query_out.at[seat]),
        wires.move(key_value.at[:, head_columns(seat)], key_value_out.at[me]),
    ]
    arrive(copies)
    for copy in kept:
        copy.wait()
    wires.finish_sends()


def to_heads(query, key_value):
    outs = [shape(QUARTER, TOKENS, 128), shape(RING, TOKENS, 128)]
    return wired_call(to_heads_kernel, outs, [query, key_value], 3, "to_heads", 38, 2)


def grad_to_heads_kernel(grad, branch, grad_out, branch_pair, sends, receives, moves):
    here = Place()
    wires = Wires(sends, receives, moves)
    _, seat, near, _ = seats(here)
    greet([(k, here.fsdp) for k in near] + [here.sibling()])
    copies = [
        wires.push(grad.at[:, head_columns(k % QUARTER)], grad_out.at[seat], (k, here.fsdp))
        for k in near
    ]
    copies.append(wires.push(branch, branch_pair.at[here.core], here.sibling()))
    kept = [
        wires.move(grad.at[:, head_columns(seat)], grad_out.at[seat]),
        wires.move(branch, branch_pair.at[here.core]),
    ]
    arrive(copies)
    for copy in kept:
        copy.wait()
    wires.finish_sends()


def grad_to_heads(grad, branch):
    outs = [shape(QUARTER, TOKENS, 128), shape(2, TOKENS, D)]
    return wired_call(grad_to_heads_kernel, outs, [grad, branch], 4, "grad_to_heads", 8, 2)


def to_tokens_kernel(query, query_out, sends, receives, moves):
    here = Place()
    wires = Wires(sends, receives, moves)
    _, seat, near, _ = seats(here)
    greet([(k, here.fsdp) for k in near])
    columns = query_out.at[:, head_columns(seat)]
    copies = [wires.push(query.at[k % QUARTER], columns, (k, here.fsdp)) for k in near]
    kept = wires.move(query.at[seat], columns)
    arrive(copies)
    kept.wait()
    wires.finish_sends()


def to_tokens(query):
    return wired_call(to_tokens_kernel, [shape(TOKENS, D)], [query], 5, "to_tokens", 7, 1)[0]


def grads_to_tokens_kernel(*refs):
    query, key_value, pieces = (refs[0], refs[1], refs[2:6])
    query_out, key_value_out, nears = (refs[6], refs[7], refs[8:12])
    here = Place()
    wires = Wires(*refs[12:])
    me, seat, near, far = seats(here)
    greet([(k, here.fsdp) for k in far])
    held = {"zh": here.zh, "zl": here.zl, "x": here.x, "y": here.y}

    def back():
        columns = query_out.at[:, head_columns(seat)]
        copies = [wires.push(query.at[k % QUARTER], columns, (k, here.fsdp)) for k in near]
        copies += [
            wires.push(key_value.at[k], key_value_out.at[me], (k, here.fsdp)) for k in far
        ]
        kept = [
            wires.move(query.at[seat], columns),
            wires.move(key_value.at[me], key_value_out.at[me]),
        ]
        for _ in range(3):
            yield
        arrive(copies)
        for copy in kept:
            copy.wait()

    def share(p):
        _, kind, _, order = WIDE[p]
        own = wires.move(pieces[p], kind.view(nears[p], held, 1))
        own.wait()
        yield from spread(
            here, wires, kind, nears[p], held, order[:2], 1, direct=FIRST_DIRECT[p]
        )

    in_turn([share(p) for p in range(4)] + [back()])
    wires.finish_sends()


def grads_to_tokens(query, key_value, pieces):
    query_grad, key_value_grad, *nears = wired_call(
        grads_to_tokens_kernel,
        [shape(TOKENS, D), shape(RING, TOKENS, 128), *(shape(*d[1:]) for d in WIDE_DIMS)],
        [query, key_value, *pieces],
        6,
        "grads_to_tokens",
        38 + 7 + 4 + 4 + 4,
        6,
    )
    return query_grad, key_value_grad, nears


def half_columns(r, core):
    return pl.ds(pl.multiple_of(r * 512 + core * 256, 256), 256)


def share_kernel(whole, halved, *refs):
    n = whole + halved
    ins, outs = (refs[:n], refs[n : 2 * n])
    here = Place()
    wires = Wires(*refs[2 * n :])
    core = here.core
    sibling = here.sibling()
    greet([sibling])
    copies, kept = ([], [])
    for source, target in zip(ins[:whole], outs[:whole]):
        copies.append(wires.push(source, target.at[core], sibling))
        kept.append(wires.move(source, target.at[core]))
    for source, target in zip(ins[whole:], outs[whole:]):
        for r in range(2):
            place = target.at[core, :, pl.ds(r * 256, 256)]
            copies.append(wires.push(source.at[:, half_columns(r, 1 - core)], place, sibling))
            kept.append(wires.move(source.at[:, half_columns(r, core)], place))
    arrive(copies)
    for copy in kept:
        copy.wait()
    wires.finish_sends()


def share(whole, halved, collective_id):
    outs = [shape(2, *a.shape, dtype=a.dtype) for a in whole]
    outs += [shape(2, a.shape[0], 512, dtype=a.dtype) for a in halved]
    count = len(whole) + 2 * len(halved)
    done = wired_call(
        functools.partial(share_kernel, len(whole), len(halved)),
        outs,
        [*whole, *halved],
        collective_id,
        "share",
        count,
        count,
    )
    return [a.reshape(2 * a.shape[1], a.shape[2]) for a in done]


def hand_over_kernel(count, *refs):
    ins, outs = (refs[:count], refs[count : 2 * count])
    here = Place()
    wires = Wires(*refs[2 * count :])
    sibling = here.sibling()
    greet([sibling])
    copies = [wires.push(i.at[1 - here.core], o, sibling) for i, o in zip(ins, outs)]
    arrive(copies)
    wires.finish_sends()


def hand_over(partials, collective_id):
    return wired_call(
        functools.partial(hand_over_kernel, len(partials)),
        [shape(*a.shape[1:], dtype=a.dtype) for a in partials],
        partials,
        collective_id,
        "hand_over",
        len(partials),
        0,
    )


def nt(left, right):
    return lax.dot_general(left, right, (((1,), (1,)), ((), ())), preferred_element_type=F32)


def nn(left, right):
    return lax.dot_general(left, right, (((1,), (0,)), ((), ())), preferred_element_type=F32)


def query_block(ref, t):
    block = ref[t].astype(F32)
    both = jnp.concatenate([block, pltpu.roll(block, 64, 1)], axis=0)
    low = lax.broadcasted_iota(jnp.int32, (128, 128), 1) < 64
    return jnp.where(low, both, 0.0)


def query_pair(ref, u):
    return [query_block(ref, 2 * u), query_block(ref, 2 * u + 1)]


def first_allowed(position, starts_ref):
    begin = jnp.zeros_like(position)
    for n in range(4):
        begin = jnp.maximum(begin, jnp.where(starts_ref[n] <= position, starts_ref[n], 0))
    return begin


def heads_beside(rows):
    low = lax.broadcasted_iota(jnp.int32, (64, 128), 1) < 64
    return jnp.where(low, rows[:64], pltpu.roll(rows[64:], 64, 1)).astype(BF16)


def attend_task(
    counts, first_block, starts_ref, order_ref, query_ref, key_value_ref, out_ref, exact_ref,
    sum_ref, value_ref, key_at_ref,
):
    def key_places(j, _):
        lane = lax.broadcasted_iota(jnp.int32, (1, 128), 1)
        block = jnp.where(lane < 64, order_ref[2 * j], order_ref[2 * j + 1])
        key_at_ref[:, pl.ds(pl.multiple_of(j * 128, 128), 128)] = block * 64 + lane % 64
        return 0

    def values(j, _):
        rows = pl.ds(pl.multiple_of(j * 256, 256), 256)
        block = pltpu.roll(key_value_ref[rows, :].astype(F32), 64, 1)
        low = lax.broadcasted_iota(jnp.int32, (256, 128), 1) < 64
        value_ref[rows, :] = jnp.where(low, block, 1.0).astype(BF16)
        return 0

    def blocks(u, _):
        queries = jnp.concatenate(query_pair(query_ref, u), axis=0).astype(BF16)
        inner = lax.broadcasted_iota(jnp.int32, (128, 1), 0) % 64
        block = first_block + 2 * u
        position = jnp.concatenate(
            [order_ref[block] * 64 + inner, order_ref[block + 1] * 64 + inner], axis=0
        )
        begin = first_allowed(position, starts_ref)

        def tile(j, total):
            rows = pl.ds(pl.multiple_of(j * KEY_TILE, KEY_TILE), KEY_TILE)
            scores = nt(queries, key_value_ref[rows, :])
            key = key_at_ref[:, rows]
            allowed = (key <= position) & (key >= begin)
            weight = jnp.where(allowed, jnp.exp2(scores * SCORE_TO_EXP2), 0.0)
            return total + nn(weight.astype(BF16), value_ref[rows, :])

        total = lax.fori_loop(0, SEQ // KEY_TILE, tile, jnp.zeros((256, 128), F32))
        attended = total / pltpu.roll(total, 64, 1)
        low = lax.broadcasted_iota(jnp.int32, (256, 128), 1) < 64
        attended = jnp.where(low, attended, 0.0)
        for n in range(2):
            rows = slice(128 * n, 128 * n + 128)
            exact_ref[2 * u + n] = attended[rows]
            out_ref[2 * u + n] = heads_beside(attended[rows])
            sum_ref[2 * u + n] = jnp.transpose(total[rows])[64:72]
        return 0

    lax.fori_loop(0, SEQ // 256, values, 0)
    lax.fori_loop(0, SEQ // 128, key_places, 0)
    first = 0
    for count in counts:
        lax.fori_loop(first, first + count, blocks, 0)
        first += count
        yield


def attend_kernel(
    starts, order, query, key_value, gate_in, up_in, down_in, attended, exact, sums, gate_all,
    up_all, down_all, value_ref, key_at_ref, sends, receives, moves,
):
    wires = Wires(sends, receives, moves)
    here = Place()
    greet_rings(here)
    in_turn(
        [
            *fetch_last(here, wires, (gate_all, up_all, down_all)),
            attend_task(
                (6, 2), here.ctx // QUARTER * 16, starts, order, query, key_value, attended, exact,
                sums, value_ref, key_at_ref,
            ),
        ]
    )
    wires.finish_sends()


def attend(starts, order, queries, key_values, wide):
    outs = [
        shape(16, 64, 128),
        shape(16, 128, 128, dtype=F32),
        shape(16, 8, 128, dtype=F32),
        *(shape(*a.shape) for a in wide),
    ]
    attended, exact, sums, gate, up, down = wired_call(
        attend_kernel,
        outs,
        [starts, order, queries, key_values, *wide],
        10,
        "attend",
        1 + 4 + 4,
        1,
        [pltpu.VMEM((SEQ, 128), BF16), pltpu.VMEM((1, SEQ), jnp.int32)],
        [SMEM] * 2 + [VMEM] * 2 + [ANY] * 3,
        [VMEM] * 3 + [ANY] * 3,
        vmem=40 * MIB,
        aliases={4 + i: 3 + i for i in range(3)},
    )
    weights = (gate.reshape(D, HALF_FF), up.reshape(D, HALF_FF), down.reshape(HALF_FF, D))
    return attended, exact, sums, weights


def attend_back_task(
    counts, first_block, starts_ref, order_ref, query_ref, key_value_ref, grad_ref, exact_ref,
    sum_ref, query_grad_ref, key_value_grad_ref, across_ref, total_ref, key_at_ref,
):
    total_ref[...] = jnp.zeros_like(total_ref)

    def key_places(j, _):
        inner = lax.broadcasted_iota(jnp.int32, (64, 1), 0)
        key_at_ref[pl.ds(pl.multiple_of(j * 64, 64), 64), :] = order_ref[j] * 64 + inner
        return 0

    def turn(j, _):
        rows = pl.ds(pl.multiple_of(j * 128, 128), 128)
        across_ref[:, rows] = jnp.transpose(key_value_ref[rows, :].astype(F32)).astype(BF16)
        return 0

    def blocks(u, _):
        queries, grads = (query_pair(query_ref, u), query_pair(grad_ref, u))
        delta = [
            jnp.sum(jnp.transpose(grad * exact_ref[2 * u + n]), axis=0, keepdims=True)
            for n, grad in enumerate(grads)
        ]
        delta = jnp.concatenate(delta, axis=1)
        total_exp2 = jnp.concatenate(
            [jnp.log2(sum_ref[2 * u + n][0:1]) for n in range(2)], axis=1
        )
        grads = [pltpu.roll(grad, 64, 1) for grad in grads]
        both = jnp.concatenate(queries + grads, axis=0).astype(BF16)
        inner = lax.broadcasted_iota(jnp.int32, (1, 128), 1) % 64
        block = first_block + 2 * u
        position = jnp.concatenate(
            [order_ref[block] * 64 + inner, order_ref[block + 1] * 64 + inner], axis=1
        )
        begin = first_allowed(position, starts_ref)

        def tile(j, query_grad):
            rows = pl.ds(pl.multiple_of(j * KEY_TILE_BACK, KEY_TILE_BACK), KEY_TILE_BACK)
            products = nt(key_value_ref[rows, :], both)
            key = key_at_ref[rows, :]
            allowed = (key <= position) & (key >= begin)
            prob = jnp.where(
                allowed, jnp.exp2(products[:, :256] * SCORE_TO_EXP2 - total_exp2), 0.0
            )
            score = (prob * (products[:, 256:] - delta)).astype(BF16)
            side = jnp.concatenate([score, prob.astype(BF16)], axis=1)
            total_ref[rows, :] += nn(side, both)
            return query_grad + nn(across_ref[:, rows], score)

        query_grad = lax.fori_loop(
            0, SEQ // KEY_TILE_BACK, tile, jnp.zeros((128, 256), F32)
        )
        for n in range(2):
            rows = jnp.transpose(query_grad[:, 128 * n : 128 * n + 128])
            query_grad_ref[2 * u + n] = heads_beside(rows * float(HEAD_SIZE) ** (-0.5))
        return 0

    def put_back(j, _):
        rows = pl.ds(pl.multiple_of(j * 256, 256), 256)
        low = lax.broadcasted_iota(jnp.int32, (256, 128), 1) < 64
        scale = jnp.where(low, float(HEAD_SIZE) ** (-0.5), 1.0)
        key_value_grad_ref[rows, :] = (total_ref[rows, :] * scale).astype(BF16)
        return 0

    lax.fori_loop(0, SEQ // 128, turn, 0)
    lax.fori_loop(0, 64, key_places, 0)
    first = 0
    for count in counts:
        lax.fori_loop(first, first + count, blocks, 0)
        first += count
        yield
    lax.fori_loop(0, SEQ // 256, put_back, 0)


def attend_back_kernel(*refs):
    attention, grads = (refs[:7], refs[7:11])
    outs, pieces = (refs[11:13], refs[13:17])
    scratch, totals, slots = (refs[17:20], refs[20:24], refs[24:36])
    here = Place()
    wires = Wires(*refs[36:])
    greet_rings(here)
    at = {"zh": here.zh, "zl": here.zl, "x": here.x, "y": here.y}

    def reduce(p):
        _, kind, order, _ = WIDE[p]
        yield from reduce_one(
            here, wires, kind, grads[p], totals[p], slots[3 * p : 3 * p + 3], order, 2
        )
        own = wires.move(kind.view(totals[p], at), pieces[p])
        yield
        own.wait()

    first_block = here.ctx // QUARTER * 16
    in_turn(
        [reduce(p) for p in range(4)]
        + [attend_back_task((3, 3, 1, 1), first_block, *attention, *outs, *scratch)]
    )
    wires.finish_sends()


def attend_back(starts, order, queries, key_values, grads, exact, sums, wide):
    ins = [starts, order, queries, key_values, grads]
    ins += [exact, sums, *(a.reshape(d) for a, d in zip(wide, WIDE_DIMS))]
    scratch = [
        pltpu.VMEM((128, SEQ), BF16),
        pltpu.VMEM((SEQ, 128), F32),
        pltpu.VMEM((SEQ, 1), jnp.int32),
    ]
    scratch += [pltpu.VMEM(d, BF16) for d in WIDE_DIMS]
    scratch += [pltpu.VMEM(s, BF16) for s in slot_shapes(WIDE)]
    query_grad, key_value_grad, *pieces = wired_call(
        attend_back_kernel,
        [shape(16, 64, 128), shape(SEQ, 128), *(shape(*d) for d in PIECE_DIMS)],
        ins,
        11,
        "attend_back",
        4 * 18,
        4 * 4,
        scratch,
        [SMEM] * 2 + [VMEM] * 5 + [ANY] * 4,
        [VMEM] * 2 + [ANY] * 4,
        vmem=58 * MIB,
    )
    return query_grad, key_value_grad, pieces


def rms_norm(values, gain_row):
    return (
        values * lax.rsqrt(jnp.mean(values * values, axis=-1, keepdims=True) + EPSILON) * gain_row
    )


def rotate(values, positions):
    half_width = values.shape[-1] // 2
    frequency = ROPE_BASE ** (-2.0 * jnp.arange(half_width, dtype=F32) / values.shape[-1])
    angles = positions.astype(F32)[:, None] * frequency[None, :]
    cosine = jnp.cos(angles)[:, None, :]
    sine_part = jnp.sin(angles)[:, None, :]
    first_half = values[..., :half_width]
    second_half = values[..., half_width:]
    return jnp.concatenate(
        [
            first_half * cosine - second_half * sine_part,
            second_half * cosine + first_half * sine_part,
        ],
        axis=-1,
    )


def outer_sum(left, right):
    return lax.dot_general(
        left, right, (((0,), (0,)), ((), ())), preferred_element_type=F32
    ).astype(BF16)


def matmul(left, right):
    return jnp.dot(left, right, preferred_element_type=F32)


def positions_at(block_order, first_row, total_row_count, half_rows):
    row_ids = first_row + jnp.arange(total_row_count, dtype=jnp.int32)
    blocks = row_ids // half_rows
    lookup = jnp.arange(block_order.shape[0], dtype=jnp.int32)
    picked = jnp.sum(jnp.where(blocks[:, None] == lookup[None, :], block_order[None, :], 0), axis=1)
    return picked * half_rows + row_ids % half_rows


def per_device(
    inputs,
    cotangent,
    qkv_weight,
    out_weight,
    gate_weight,
    up_weight,
    down_weight,
    gain_attn,
    gain_query,
    gain_key,
    gain_ffn,
    block_order,
    doc_starts,
):
    cycle_index = lax.axis_index("ctx")
    core = lax.axis_index("fsdp") % 2
    qkv_all, out_all, wide = gather(
        qkv_weight, out_weight, gate_weight, up_weight, down_weight
    )
    places = (doc_starts[0], block_order)
    positions = positions_at(block_order, cycle_index * TOKENS, TOKENS, TOKENS // 2)

    resid_in = inputs[0].astype(F32)
    normed, norm_in_pull = jax.vjp(rms_norm, resid_in, gain_attn)
    normed_low = normed.astype(BF16)
    projected = matmul(normed_low, qkv_all)
    split_position = (QUERY_HEADS + KEY_VALUE_HEADS) * HEAD_SIZE

    def query_key(leading_columns, scale_query, scale_key):
        queries = leading_columns[:, : QUERY_HEADS * HEAD_SIZE].reshape(
            TOKENS, QUERY_HEADS, HEAD_SIZE
        )
        keys = leading_columns[:, QUERY_HEADS * HEAD_SIZE :].reshape(
            TOKENS, KEY_VALUE_HEADS, HEAD_SIZE
        )
        return (
            rotate(rms_norm(queries, scale_query), positions),
            rotate(rms_norm(keys, scale_key), positions),
        )

    (queries, keys), qk_pull = jax.vjp(
        query_key, projected[:, :split_position], gain_query, gain_key
    )
    values = projected[:, split_position:].reshape(TOKENS, KEY_VALUE_HEADS, HEAD_SIZE)
    key_values = jnp.concatenate([keys, values], axis=-1).astype(BF16).reshape(TOKENS, D)
    query_part, key_value_part = to_heads(queries.astype(BF16).reshape(TOKENS, D), key_values)
    query_part = query_part.reshape(16, 64, 128)
    key_value_part = key_value_part.reshape(SEQ, 128)
    attended, exact, sums, (gate_all, up_all, down_all) = attend(
        *places, query_part, key_value_part, wide
    )
    attended_low = to_tokens(attended.reshape(QUARTER, TOKENS, 128))

    residual = resid_in + matmul(attended_low, out_all)
    normed_ffn, norm_ffn_pull = jax.vjp(rms_norm, residual, gain_ffn)
    grad_out = cotangent[0]
    ffn_pair, cotangent_pair, normed_half, attended_half = share(
        [normed_ffn.astype(BF16), grad_out], [normed_low, attended_low], 7
    )
    gate_proj = matmul(ffn_pair, gate_all)
    up_proj = matmul(ffn_pair, up_all)
    hidden, gating_pull = jax.vjp(
        lambda gate_in, up_in: jax.nn.silu(gate_in) * up_in, gate_proj, up_proj
    )
    hidden_low = hidden.astype(BF16)
    out_partial = matmul(hidden_low, down_all).reshape(2, TOKENS, D)
    grad_hidden = matmul(cotangent_pair, down_all.T)
    grad_gate, grad_up = gating_pull(grad_hidden)
    gate_low = grad_gate.astype(BF16)
    up_low = grad_up.astype(BF16)
    ffn_partial = (matmul(gate_low, gate_all.T) + matmul(up_low, up_all.T)).reshape(2, TOKENS, D)
    out_rest, ffn_rest = hand_over([out_partial, ffn_partial], 8)

    def mine(pair):
        return lax.dynamic_index_in_dim(pair, core, 0, keepdims=False)

    outputs = residual + mine(out_partial) + out_rest
    grad_resid_ffn, grad_gain_ffn = norm_ffn_pull(mine(ffn_partial) + ffn_rest)
    grad_resid = grad_out.astype(F32) + grad_resid_ffn
    branch_low = grad_resid.astype(BF16)
    grad_attended = matmul(branch_low, out_all.T).astype(BF16)
    grad_part, branch_pair = grad_to_heads(grad_attended, branch_low)
    query_grad, key_value_grad, pieces = attend_back(
        *places,
        query_part,
        key_value_part,
        grad_part.reshape(16, 64, 128),
        exact,
        sums,
        (
            outer_sum(ffn_pair, gate_low),
            outer_sum(ffn_pair, up_low),
            outer_sum(hidden_low, cotangent_pair),
            outer_sum(attended_half, branch_pair.reshape(2 * TOKENS, D)),
        ),
    )
    query_grad, key_value_grad, nears = grads_to_tokens(
        query_grad.reshape(QUARTER, TOKENS, 128),
        key_value_grad.reshape(RING, TOKENS, 128),
        pieces,
    )
    key_value_grad = key_value_grad.reshape(4, KEY_VALUE_HEADS, TOKENS, 128)
    key_value_grad = jnp.transpose(jnp.sum(key_value_grad.astype(F32), axis=0), (1, 0, 2))
    grad_front, grad_gain_query, grad_gain_key = qk_pull(
        (
            query_grad.astype(F32).reshape(TOKENS, QUERY_HEADS, HEAD_SIZE),
            key_value_grad[..., :HEAD_SIZE],
        )
    )
    grad_values = key_value_grad[..., HEAD_SIZE:].reshape(TOKENS, KEY_VALUE_HEADS * HEAD_SIZE)
    grad_projected = jnp.concatenate([grad_front, grad_values], axis=1).astype(BF16)
    grad_normed = matmul(grad_projected, qkv_all.T)
    grad_input_norm, grad_gain_attn = norm_in_pull(grad_normed)
    grad_inputs = (grad_resid + grad_input_norm).astype(BF16)

    (projected_pair,) = share([grad_projected], [], 9)
    gains = jnp.concatenate([grad_gain_attn, grad_gain_ffn, grad_gain_query, grad_gain_key])
    gains = jnp.pad(gains, (0, 24 * 128 - gains.shape[0])).reshape(24, 128)
    grad_qkv, grad_out_weight, grad_gate_weight, grad_up_weight, grad_down, gains = reduce_weights(
        nears, outer_sum(normed_half, projected_pair), gains
    )
    gains = gains.reshape(-1)
    return (
        outputs.astype(BF16)[None],
        grad_inputs[None],
        grad_qkv.astype(F32),
        grad_out_weight.astype(F32),
        grad_gate_weight.astype(F32),
        grad_up_weight.astype(F32),
        grad_down.astype(F32),
        gains[:D],
        gains[2 * D : 2 * D + HEAD_SIZE],
        gains[2 * D + HEAD_SIZE : 2 * D + 2 * HEAD_SIZE],
        gains[D : 2 * D],
    )


def solution(mesh):
    in_specs = (
        P("fsdp", "ctx", None),
        P("fsdp", "ctx", None),
        P("fsdp", None),
        P("fsdp", None),
        P("fsdp", None),
        P("fsdp", None),
        P("fsdp", None),
        P(),
        P(),
        P(),
        P(),
        P(),
        P("fsdp", None),
    )
    out_specs = (
        P("fsdp", "ctx", None),
        P("fsdp", "ctx", None),
        P("fsdp", None),
        P("fsdp", None),
        P("fsdp", None),
        P("fsdp", None),
        P("fsdp", None),
        P(),
        P(),
        P(),
        P(),
    )
    return jax.shard_map(
        per_device, mesh=mesh, in_specs=in_specs, out_specs=out_specs, check_vma=False
    )
```

profile of v0, /device:TPU:0, one launch (start us, length us, event | category | flops | bytes accessed | tf_op | source)
XLA Modules:
  0.0 414.7 jit_solution(5083839476340034141)
XLA Ops:
  7.9 38.1 %gather.1 = (bf16[2,2,4,4,16,2048]{5,4,3,2,1,0:T(8,128)(2,1)S(1)}, bf16[2,2,4,4,16,1024]{5,4,3,2,1,0:T(8,128)(2,1)S(1)}, bf16[2,2,4,4,16,2304]{5,4,3,2,1,0:T(8,1...) custom-call(bf16[4,4,16,2048]{3,2,1,0:T(8,128)(2,1)S(1)} %bitcast.184, ...), custom_call_target="tpu_custom_call" | custom-call | tf_op jit(solution)/shard_map/gather/pallas_call | solution.py:105
  46.2 1.9 copy-done.9
  58.1 1.9 slice.96
  65.4 21.0 %to_heads.1 = (bf16[8,128,128]{2,1,0:T(8,128)(2,1)S(1)}, bf16[32,128,128]{2,1,0:T(8,128)(2,1)S(1)}) custom-call(bf16[128,1024]{1,0:T(8,128)(2,1)S(1)} %copy.93.query, bf16[128,1024]{1,0:T(8,128)(2,1)S(1)} %copy.106.key_value), custom_call_target="tpu_custom_call" | custom-call | tf_op jit(solution)/shard_map/to_heads/pallas_call | solution.py:105
  86.4 2.8 copy-done.7
  89.2 2.3 copy-done.8
  91.6 37.8 %attend.1 = (bf16[16,64,128]{2,1,0:T(8,128)(2,1)S(1)}, f32[16,128,128]{2,1,0:T(8,128)S(1)}, f32[16,8,128]{2,1,0:T(8,128)S(1)}, bf16[2,2,4,4,16,2304]{5,4,3,2,1,0...) custom-call(s32[4]{0:T(128)S(1)} %bitcast.195, ...), custom_call_target="tpu_custom_call", output_to_operand_aliasing={{3}: (4, {}), {4}: (5, {}), {5}: (6, {})} | custom-call | tf_op jit(solution)/shard_map/attend/pallas_call | solution.py:105
  129.4 7.7 %to_tokens.1.refs_3_ = bf16[128,1024]{1,0:T(8,128)(2,1)S(1)} custom-call(bf16[8,128,128]{2,1,0:T(8,128)(2,1)S(1)} %bitcast.191), custom_call_target="tpu_custom_call" | custom-call | tf_op jit(solution)/shard_map/to_tokens/pallas_call | solution.py:105
  138.3 2.5 share.2
  143.6 2.4 multiply_convert_fusion
  150.4 2.8 hand_over.1
  155.8 2.2 multiply_reduce_fusion.2
  160.2 7.9 %grad_to_heads.1 = (bf16[8,128,128]{2,1,0:T(8,128)(2,1)S(1)}, bf16[2,128,1024]{2,1,0:T(8,128)(2,1)S(1)}) custom-call(bf16[128,1024]{1,0:T(8,128)(2,1)S(1)} %convolution_convert_fusion.3.grad, bf16[128,1024]{1,0:T(8,128)(2,1)S(1)} %fusion.35.branch), custom_call_target="tpu_custom_call" | custom-call | tf_op jit(solution)/shard_map/grad_to_heads/pallas_call | solution.py:105
  169.6 3.6 convolution_convert_fusion
  173.2 3.6 convolution_convert_fusion.1
  176.8 3.6 convolution_convert_fusion.2
  180.5 77.3 %attend_back.1 = (bf16[16,64,128]{2,1,0:T(8,128)(2,1)}, bf16[4096,128]{1,0:T(8,128)(2,1)}, bf16[16,2304]{1,0:T(8,128)(2,1)}, bf16[16,2304]{1,0:T(8,128)(2,1)}, b...) custom-call(s32[4]{0:T(128)} %bitcast.194, s32[64]{0:T(128)} %refs_1_.1, bf16[16,64,128]{2,1,0:T(8,128)(2,1)} %bitcast.183, ...), custom_call_target="tpu_custom_call" | custom-call | tf_op jit(solution)/shard_map/attend_back/pallas_call | solution.py:105
  263.4 31.1 %grads_to_tokens.1 = (bf16[128,1024]{1,0:T(8,128)(2,1)S(1)}, bf16[32,128,128]{2,1,0:T(8,128)(2,1)S(1)}, bf16[2,4,4,16,2304]{4,3,2,1,0:T(8,128)(2,1)S(1)}, bf16[2...) custom-call(bf16[8,128,128]{2,1,0:T(8,128)(2,1)S(1)} %bitcast.192, ...), custom_call_target="tpu_custom_call" | custom-call | tf_op jit(solution)/shard_map/grads_to_tokens/pallas_call | solution.py:105
  298.2 1.9 copy.97
  300.2 1.8 copy.98
  302.0 1.9 copy.99
  305.0 2.0 multiply_reduce_fusion.1
  308.0 2.0 copy.100
  310.0 1.9 add_convert_fusion
  311.9 1.9 slice.126
  315.7 5.4 %fusion.11 = (f32[1024]{0:T(1024)}, f32[128]{0:T(128)}, f32[128,1024]{1,0:T(8,128)}) fusion(bf16[1,128,1024]{2,1,0:T(8,128)(2,1)} %param.13, f32[128]{0:T(128)S(1)} %copy-done.89, f32[1024]{0:T(1024)S(1)} %copy-done.76, bf16[1024,2048]{1,0:T(8,128)(2,1)} %bitcast.173, bf16[128,512]{1,0:T(8,128)(2,1)} %copy.102, bf16[128,1536]{1,0:T(8,128)(2,1)} %add_convert_fusion), kind=kOutput, calls=%fused_computation.39 | convolution fusion | flops 538835840 | bytes 5514240 | tf_op jit(solution)/shard_map/dot_general | solution.py:1114
  322.9 2.0 share.3
  326.6 66.1 %reduce_weights.1 = (bf16[2,4,4,16,2304]{4,3,2,1,0:T(8,128)(2,1)S(1)}, bf16[2,4,4,16,2304]{4,3,2,1,0:T(8,128)(2,1)S(1)}, bf16[4,2,144,1024]{3,2,1,0:T(8,128)(2,1...) custom-call(bf16[2,4,4,16,2304]{4,3,2,1,0:T(8,128)(2,1)S(1)} %copy-d, ...), custom_call_target="tpu_custom_call", output_to_operand_aliasing={{0}: (0, {}), {1}: (1, {}), {2}: (2, {}), {3}: (3, {})} | custom-call | tf_op jit(solution)/shard_map/reduce_weights/pallas_call | solution.py:105
  396.8 1.8 bitcast_select_fusion.1
  398.8 2.7 maximum_convert_fusion.1
  403.4 2.7 maximum_convert_fusion
  406.1 2.9 bitcast_convert_fusion.1
  (265 shorter events, 64.9 us)
Async XLA Ops:
  7.9 38.2 %copy-start.50 = (bf16[1,128,1024]{2,1,0:T(8,128)(2,1)S(1)}, bf16[1,128,1024]{2,1,0:T(8,128)(2,1)}, u32[]{:S(2)}) copy-start(bf16[1,128,1024]{2,1,0:T(8,128)(2,1)} %param.13) | copy-start | bytes 786436
  7.9 40.2 %copy-start.74 = (f32[1024]{0:T(1024)S(1)}, f32[1024]{0:T(1024)}, u32[]{:S(2)}) copy-start(f32[1024]{0:T(1024)} %param.20) | copy-start | bytes 12292
  51.4 5.7 %copy-start.72 = (f32[128,8]{0,1:T(8,128)}, f32[128,8]{0,1:T(8,128)S(1)}, u32[]{:S(2)}) copy-start(f32[128,8]{0,1:T(8,128)S(1)} %fusion.29) | copy-start | bytes 12292
  51.6 6.3 %copy-start.48 = (f32[128,8,64]{2,0,1:T(8,128)}, f32[128,8,64]{2,0,1:T(8,128)S(1)}, u32[]{:S(2)}) copy-start(f32[128,8,64]{2,0,1:T(8,128)S(1)} %copy.86) | copy-start | bytes 786436
  60.0 26.5 %copy-start.41 = (s32[1,4]{1,0:T(1,128)S(1)}, s32[1,4]{1,0:T(1,128)}, u32[]{:S(2)}) copy-start(s32[1,4]{1,0:T(1,128)} %param.25) | copy-start | bytes 52
  86.4 43.0 %copy-start.10 = (bf16[32,128,128]{2,1,0:T(8,128)(2,1)}, bf16[32,128,128]{2,1,0:T(8,128)(2,1)S(1)}, u32[]{:S(2)}) copy-start(bf16[32,128,128]{2,1,0:T(8,128)(2,1)S(1)} %get-tuple-element.54) | copy-start | bytes 3145732
  86.4 43.0 %copy-start.21 = (bf16[8,128,128]{2,1,0:T(8,128)(2,1)}, bf16[8,128,128]{2,1,0:T(8,128)(2,1)S(1)}, u32[]{:S(2)}) copy-start(bf16[8,128,128]{2,1,0:T(8,128)(2,1)S(1)} %get-tuple-element.53) | copy-start | bytes 786436
  129.4 8.6 %copy-start.23 = (f32[16,128,128]{2,1,0:T(8,128)}, f32[16,128,128]{2,1,0:T(8,128)S(1)}, u32[]{:S(2)}) copy-start(f32[16,128,128]{2,1,0:T(8,128)S(1)} %get-tuple-element.68.refs_5_) | copy-start | bytes 3145732
  129.4 8.6 %copy-start.39 = (f32[16,8,128]{2,1,0:T(8,128)}, f32[16,8,128]{2,1,0:T(8,128)S(1)}, u32[]{:S(2)}) copy-start(f32[16,8,128]{2,1,0:T(8,128)S(1)} %get-tuple-element.69.refs_6_) | copy-start | bytes 196612
  129.4 8.3 %copy-start.70 = (f32[1024]{0:T(1024)S(1)}, f32[1024]{0:T(1024)}, u32[]{:S(2)}) copy-start(f32[1024]{0:T(1024)} %param.23) | copy-start | bytes 12292
  129.4 8.3 %copy-start.75 = (f32[1024]{0:T(1024)S(1)}, f32[1024]{0:T(1024)}, u32[]{:S(2)}) copy-start(f32[1024]{0:T(1024)} %param.20) | copy-start | bytes 12292
  129.4 8.3 %copy-start.88 = (f32[128]{0:T(128)S(1)}, f32[128]{0:T(128)}, u32[]{:S(2)}) copy-start(f32[128]{0:T(128)} %copy-done.87) | copy-start | bytes 1540
  137.7 4.5 %copy-start.45 = (f32[128,1024]{1,0:T(8,128)}, f32[128,1024]{1,0:T(8,128)S(1)}, u32[]{:S(2)}) copy-start(f32[128,1024]{1,0:T(8,128)S(1)} %get-tuple-element.134) | copy-start | bytes 1572868
  148.9 6.8 %copy-start.82 = (f32[128]{0:T(128)S(1)}, f32[128]{0:T(128)}, u32[]{:S(2)}) copy-start(f32[128]{0:T(128)} %copy-done.81) | copy-start | bytes 1540
  159.4 10.2 %copy-start.31 = (bf16[2,128,1024]{2,1,0:T(8,128)(2,1)S(1)}, bf16[2,128,1024]{2,1,0:T(8,128)(2,1)}, u32[]{:S(2)}) copy-start(bf16[2,128,1024]{2,1,0:T(8,128)(2,1)} %copy-done.30) | copy-start | bytes 1572868
  159.4 10.2 %copy-start.57 = (bf16[256,2304]{1,0:T(8,128)(2,1)S(1)}, bf16[256,2304]{1,0:T(8,128)(2,1)}, u32[]{:S(2)}) copy-start(bf16[256,2304]{1,0:T(8,128)(2,1)} %copy-done.56) | copy-start | bytes 3538948
  168.1 5.1 %copy-start.33 = (bf16[8,128,128]{2,1,0:T(8,128)(2,1)}, bf16[8,128,128]{2,1,0:T(8,128)(2,1)S(1)}, u32[]{:S(2)}) copy-start(bf16[8,128,128]{2,1,0:T(8,128)(2,1)S(1)} %get-tuple-element.67) | copy-start | bytes 786436
  263.4 31.6 %copy-start.49 = (f32[128,8,64]{2,0,1:T(8,128)S(1)}, f32[128,8,64]{2,0,1:T(8,128)}, u32[]{:S(2)}) copy-start(f32[128,8,64]{2,0,1:T(8,128)} %copy-done.48) | copy-start | bytes 786436
  263.4 31.6 %copy-start.73 = (f32[128,8]{0,1:T(8,128)S(1)}, f32[128,8]{0,1:T(8,128)}, u32[]{:S(2)}) copy-start(f32[128,8]{0,1:T(8,128)} %copy-done.72) | copy-start | bytes 12292
  263.4 31.6 %copy-start.85 = (f32[64]{0:T(128)S(1)}, f32[64]{0:T(128)}, u32[]{:S(2)}) copy-start(f32[64]{0:T(128)} %param.22) | copy-start | bytes 772
  296.8 7.1 %copy-start.65 = (f32[128,32]{0,1:T(8,128)S(1)}, f32[128,32]{0,1:T(8,128)}, u32[]{:S(2)}) copy-start(f32[128,32]{0,1:T(8,128)} %copy-done.64) | copy-start | bytes 49156
  296.8 7.1 %copy-start.67 = (f32[128,32]{0,1:T(8,128)S(1)}, f32[128,32]{0,1:T(8,128)}, u32[]{:S(2)}) copy-start(f32[128,32]{0,1:T(8,128)} %copy-done.66) | copy-start | bytes 49156
  296.9 8.1 %copy-start.86 = (f32[64]{0:T(128)S(1)}, f32[64]{0:T(128)}, u32[]{:S(2)}) copy-start(f32[64]{0:T(128)} %param.21) | copy-start | bytes 772
  298.2 8.8 %copy-start.69 = (f32[128,16]{0,1:T(8,128)S(1)}, f32[128,16]{0,1:T(8,128)}, u32[]{:S(2)}) copy-start(f32[128,16]{0,1:T(8,128)} %copy-done.68) | copy-start | bytes 24580
  307.0 8.6 %copy-start.76 = (f32[1024]{0:T(1024)S(1)}, f32[1024]{0:T(1024)}, u32[]{:S(2)}) copy-start(f32[1024]{0:T(1024)} %param.20) | copy-start | bytes 12292
  308.0 7.7 %copy-start.89 = (f32[128]{0:T(128)S(1)}, f32[128]{0:T(128)}, u32[]{:S(2)}) copy-start(f32[128]{0:T(128)} %copy-done.87) | copy-start | bytes 1540
  315.7 5.4 %copy-start.80 = (f32[1024]{0:T(1024)S(1)}, f32[1024]{0:T(1024)}, u32[]{:S(2)}) copy-start(f32[1024]{0:T(1024)} %get-tuple-element.95) | copy-start | bytes 12292
  315.7 6.2 %copy-start.63 = (bf16[128,512]{1,0:T(8,128)(2,1)S(1)}, bf16[128,512]{1,0:T(8,128)(2,1)}, u32[]{:S(2)}) copy-start(bf16[128,512]{1,0:T(8,128)(2,1)} %copy.102) | copy-start | bytes 393220
  409.0 4.1 copy-start.29
  409.0 4.1 copy-start.47
  409.0 4.1 copy-start.51
  409.0 4.1 copy-start.54
  (67 other events, 139.2 us)
where the time goes:
time: 422 us; the launch traced here: 415 us
  Pallas kernels  294 us (70%)
  local copies, waits for them, and re-layouts  54.5 us (13%)
  other arithmetic  33.7 us (8%)
  matrix products  30 us (7%)
    pallas_call x11, Pallas kernels, wired_call(): pl.pallas_call(kernel, out_shape=outs, in_specs=[ANY] * len(ins) if in_sp...  294 us
    unnamed x198, local copies, waits for them, and re-layouts  32.7 us
    dot_general x10, matrix products, matmul(): return jnp.dot(left, right, preferred_element_type=F32)  16.9 us
    dot_general x5, matrix products, outer_sum(): lax.dot_general(left, right, (((0,), (0,)), ((), ())), preferred_element_...  13.1 us

commit v1 on v0

--- a/solution.py
+++ b/solution.py
@@ -28,6 +28,7 @@
 
 MESH = pl.DeviceIdType.MESH
 ANY = pl.BlockSpec(memory_space=pl.ANY)
+HBM = pl.BlockSpec(memory_space=pltpu.MemorySpace.HBM)
 VMEM = pl.BlockSpec(memory_space=pltpu.VMEM)
 SMEM = pl.BlockSpec(memory_space=pltpu.SMEM)
 BF16 = jnp.bfloat16
@@ -229,6 +230,13 @@
 def in_turn(tasks):
     while tasks:
         tasks = [task for task in tasks if next(task, "over") != "over"]
+
+
+def later(task, rounds):
+    next(task)
+    for _ in range(rounds + 1):
+        yield
+    yield from task
 
 
 def spread(here, wires, kind, ref, at, order, skip=0, direct=""):
@@ -394,16 +402,21 @@
         "gather",
         3 * 8 + 9 + 6 + 5 + 6,
         7,
+        in_specs=[HBM] * 5,
+        out_specs=[ANY] * 2 + [HBM] * 3,
     )
     return qkv.reshape(D, 2048), out.reshape(D, D), wide
 
 
 def fetch_last(here, wires, wide):
+    tasks = []
     for (kind, order), whole in zip(WIDE_FETCH, wide):
         at = {"zh": 1 - here.zh, "zl": here.zl, "x": here.x, "y": here.y}
         for axis in order[:2]:
             at = without(at, axis)
-        yield spread(here, wires, kind, whole, at, order[2:])
+        task = spread(here, wires, kind, whole, at, order[2:])
+        tasks.append(later(task, 1) if order[2] == "z" else task)
+    return tasks
 
 
 WIDE = (
@@ -580,7 +593,11 @@
             yield
             arrive(copies)
 
-    in_turn([narrow(p) for p in range(2)] + [wide(p) for p in range(4)] + [all_gains()])
+    in_turn(
+        [narrow(p) for p in range(2)]
+        + [later(wide(p), rounds) for p, rounds in ((1, 2), (2, 2), (3, 1), (0, 4))]
+        + [all_gains()]
+    )
     wires.finish_sends()
 
 
@@ -604,8 +621,8 @@
         10 + 2 * (18 + 7) + 1 + 3 * 4 + 2,
         2 * 4,
         scratch,
-        [ANY] * 5 + [VMEM],
-        [ANY] * 7 + [VMEM],
+        [HBM] * 4 + [ANY] + [VMEM],
+        [HBM] * 7 + [VMEM],
         vmem=40 * MIB,
         aliases={i: i for i in range(4)},
     )
@@ -757,6 +774,8 @@
         "grads_to_tokens",
         38 + 7 + 4 + 4 + 4,
         6,
+        in_specs=[ANY] * 2 + [HBM] * 4,
+        out_specs=[ANY] * 2 + [HBM] * 4,
     )
     return query_grad, key_value_grad, nears
 
@@ -921,7 +940,7 @@
     greet_rings(here)
     in_turn(
         [
-            *fetch_last(here, wires, (gate_all, up_all, down_all)),
+            *fetch_last(here, wires, (gate_all, up_all, down_all))[::-1],
             attend_task(
                 (6, 2), here.ctx // QUARTER * 16, starts, order, query, key_value, attended, exact,
                 sums, value_ref, key_at_ref,
@@ -947,8 +966,8 @@
         1 + 4 + 4,
         1,
         [pltpu.VMEM((SEQ, 128), BF16), pltpu.VMEM((1, SEQ), jnp.int32)],
-        [SMEM] * 2 + [VMEM] * 2 + [ANY] * 3,
-        [VMEM] * 3 + [ANY] * 3,
+        [SMEM] * 2 + [VMEM] * 2 + [HBM] * 3,
+        [VMEM] * 3 + [HBM] * 3,
         vmem=40 * MIB,
         aliases={4 + i: 3 + i for i in range(3)},
     )
@@ -1074,11 +1093,135 @@
         4 * 18,
         4 * 4,
         scratch,
-        [SMEM] * 2 + [VMEM] * 5 + [ANY] * 4,
-        [VMEM] * 2 + [ANY] * 4,
+        [SMEM] * 2 + [VMEM] * 5 + [HBM] * 4,
+        [VMEM] * 2 + [HBM] * 4,
         vmem=58 * MIB,
     )
     return query_grad, key_value_grad, pieces
+
+
+def low_lanes():
+    return lax.broadcasted_iota(jnp.int32, (TOKENS, 128), 1) < 64
+
+
+def head_mean(values):
+    low = low_lanes()
+    first = jnp.sum(jnp.where(low, values, 0.0), axis=1, keepdims=True)
+    second = jnp.sum(jnp.where(low, 0.0, values), axis=1, keepdims=True)
+    return jnp.where(low, first, second) * (1.0 / HEAD_SIZE)
+
+
+def other_half(values):
+    first = lax.broadcasted_iota(jnp.int32, (TOKENS, 128), 1) % 64 < 32
+    return jnp.where(first, pltpu.roll(values, 96, 1), pltpu.roll(values, 32, 1))
+
+
+def chunk(j):
+    return slice(128 * j, 128 * j + 128)
+
+
+def project_kernel(
+    x_ref, gain_ref, weight_ref, query_gain_ref, key_gain_ref, cosine_ref, sine_ref, normed_ref,
+    query_ref, key_value_ref, projected_ref,
+):
+    x = x_ref[...].astype(F32)
+    normed = x * lax.rsqrt(jnp.mean(x * x, axis=-1, keepdims=True) + EPSILON) * gain_ref[...]
+    normed_ref[...] = normed.astype(BF16)
+    projected = nn(normed_ref[...], weight_ref[...])
+    projected_ref[...] = projected[:, :1536]
+    low = low_lanes()
+
+    def turned(j, gain):
+        values = projected[:, chunk(j)]
+        values = values * lax.rsqrt(head_mean(values * values) + EPSILON) * gain
+        return values * cosine_ref[...] + other_half(values) * sine_ref[...]
+
+    for j in range(8):
+        query_ref[:, chunk(j)] = turned(j, query_gain_ref[...]).astype(BF16)
+    for j in range(4):
+        keys = turned(8 + j, key_gain_ref[...])
+        values = projected[:, chunk(12 + j)]
+        first = jnp.where(low, keys, pltpu.roll(values, 64, 1))
+        second = jnp.where(low, pltpu.roll(keys, 64, 1), values)
+        key_value_ref[:, chunk(2 * j)] = first.astype(BF16)
+        key_value_ref[:, chunk(2 * j + 1)] = second.astype(BF16)
+
+
+def project(x, gain, weight, query_gain, key_gain, cosine, sine):
+    return pl.pallas_call(
+        project_kernel,
+        out_shape=[
+            shape(TOKENS, D),
+            shape(TOKENS, D),
+            shape(TOKENS, D),
+            shape(TOKENS, 1536, dtype=F32),
+        ],
+        in_specs=[VMEM] * 7,
+        out_specs=[VMEM] * 4,
+        compiler_params=pltpu.CompilerParams(vmem_limit_bytes=32 * MIB),
+        name="project",
+    )(x, gain, weight, query_gain, key_gain, cosine, sine)
+
+
+def project_back_kernel(
+    query_grad_ref, key_value_grad_ref, projected_ref, x_ref, grad_resid_ref, gain_ref, weight_ref,
+    query_gain_ref, key_gain_ref, cosine_ref, sine_ref, ffn_gain_grad_ref, grad_projected_ref,
+    grad_inputs_ref, gains_ref,
+):
+    low = low_lanes()
+
+    def back(j, grad, gain):
+        grad = grad * cosine_ref[...] + other_half(grad * sine_ref[...])
+        values = projected_ref[:, chunk(j)]
+        scale = lax.rsqrt(head_mean(values * values) + EPSILON)
+        unit = values * scale
+        gain_grad = jnp.sum(grad * unit, axis=0, keepdims=True)
+        grad = grad * gain
+        grad = scale * (grad - unit * head_mean(grad * unit))
+        grad_projected_ref[:, chunk(j)] = grad.astype(BF16)
+        return gain_grad
+
+    query_gain_grad = jnp.zeros((1, 128), F32)
+    for j in range(8):
+        grad = query_grad_ref[:, chunk(j)].astype(F32)
+        query_gain_grad += back(j, grad, query_gain_ref[...])
+    key_gain_grad = jnp.zeros((1, 128), F32)
+    for j in range(4):
+        first, second = [
+            sum(key_value_grad_ref[8 * q + 2 * j + n].astype(F32) for q in range(4))
+            for n in range(2)
+        ]
+        keys = jnp.where(low, first, pltpu.roll(second, 64, 1))
+        values = jnp.where(low, pltpu.roll(first, 64, 1), second)
+        key_gain_grad += back(8 + j, keys, key_gain_ref[...])
+        grad_projected_ref[:, chunk(12 + j)] = values.astype(BF16)
+
+    grad = nt(grad_projected_ref[...], weight_ref[...])
+    x = x_ref[...].astype(F32)
+    scale = lax.rsqrt(jnp.mean(x * x, axis=-1, keepdims=True) + EPSILON)
+    unit = x * scale
+    gain_grad = jnp.sum(grad * unit, axis=0, keepdims=True)
+    grad = grad * gain_ref[...]
+    grad = scale * (grad - unit * jnp.mean(grad * unit, axis=-1, keepdims=True))
+    grad_inputs_ref[...] = (grad_resid_ref[...] + grad).astype(BF16)
+
+    gains_ref[...] = jnp.zeros_like(gains_ref)
+    for j in range(8):
+        gains_ref[j : j + 1, :] = gain_grad[:, chunk(j)]
+        gains_ref[8 + j : 9 + j, :] = ffn_gain_grad_ref[:, chunk(j)]
+    gains_ref[16:17, :] = query_gain_grad + pltpu.roll(query_gain_grad, 64, 1)
+    gains_ref[17:18, :] = key_gain_grad + pltpu.roll(key_gain_grad, 64, 1)
+
+
+def project_back(*ins):
+    return pl.pallas_call(
+        project_back_kernel,
+        out_shape=[shape(TOKENS, 2048), shape(TOKENS, D), shape(24, 128, dtype=F32)],
+        in_specs=[VMEM] * 12,
+        out_specs=[VMEM] * 3,
+        compiler_params=pltpu.CompilerParams(vmem_limit_bytes=40 * MIB),
+        name="project_back",
+    )(*ins)
 
 
 def rms_norm(values, gain_row):
@@ -1087,21 +1230,12 @@
     )
 
 
-def rotate(values, positions):
-    half_width = values.shape[-1] // 2
-    frequency = ROPE_BASE ** (-2.0 * jnp.arange(half_width, dtype=F32) / values.shape[-1])
+def rope_tables(positions):
+    lane = jnp.arange(128, dtype=jnp.int32)
+    frequency = ROPE_BASE ** (-2.0 * (lane % 32).astype(F32) / HEAD_SIZE)
     angles = positions.astype(F32)[:, None] * frequency[None, :]
-    cosine = jnp.cos(angles)[:, None, :]
-    sine_part = jnp.sin(angles)[:, None, :]
-    first_half = values[..., :half_width]
-    second_half = values[..., half_width:]
-    return jnp.concatenate(
-        [
-            first_half * cosine - second_half * sine_part,
-            second_half * cosine + first_half * sine_part,
-        ],
-        axis=-1,
-    )
+    sign = jnp.where(lane % 64 < 32, -1.0, 1.0)
+    return jnp.cos(angles), jnp.sin(angles) * sign[None, :]
 
 
 def outer_sum(left, right):
@@ -1146,29 +1280,13 @@
     positions = positions_at(block_order, cycle_index * TOKENS, TOKENS, TOKENS // 2)
 
     resid_in = inputs[0].astype(F32)
-    normed, norm_in_pull = jax.vjp(rms_norm, resid_in, gain_attn)
-    normed_low = normed.astype(BF16)
-    projected = matmul(normed_low, qkv_all)
-    split_position = (QUERY_HEADS + KEY_VALUE_HEADS) * HEAD_SIZE
-
-    def query_key(leading_columns, scale_query, scale_key):
-        queries = leading_columns[:, : QUERY_HEADS * HEAD_SIZE].reshape(
-            TOKENS, QUERY_HEADS, HEAD_SIZE
-        )
-        keys = leading_columns[:, QUERY_HEADS * HEAD_SIZE :].reshape(
-            TOKENS, KEY_VALUE_HEADS, HEAD_SIZE
-        )
-        return (
-            rotate(rms_norm(queries, scale_query), positions),
-            rotate(rms_norm(keys, scale_key), positions),
-        )
-
-    (queries, keys), qk_pull = jax.vjp(
-        query_key, projected[:, :split_position], gain_query, gain_key
-    )
-    values = projected[:, split_position:].reshape(TOKENS, KEY_VALUE_HEADS, HEAD_SIZE)
-    key_values = jnp.concatenate([keys, values], axis=-1).astype(BF16).reshape(TOKENS, D)
-    query_part, key_value_part = to_heads(queries.astype(BF16).reshape(TOKENS, D), key_values)
+    gain_row = gain_attn.reshape(1, D)
+    head_gains = [jnp.concatenate([g, g]).reshape(1, 128) for g in (gain_query, gain_key)]
+    tables = rope_tables(positions)
+    normed_low, queries, key_values, projected = project(
+        inputs[0], gain_row, qkv_all, *head_gains, *tables
+    )
+    query_part, key_value_part = to_heads(queries, key_values)
     query_part = query_part.reshape(16, 64, 128)
     key_value_part = key_value_part.reshape(SEQ, 128)
     attended, exact, sums, (gate_all, up_all, down_all) = attend(
@@ -1224,23 +1342,20 @@
         key_value_grad.reshape(RING, TOKENS, 128),
         pieces,
     )
-    key_value_grad = key_value_grad.reshape(4, KEY_VALUE_HEADS, TOKENS, 128)
-    key_value_grad = jnp.transpose(jnp.sum(key_value_grad.astype(F32), axis=0), (1, 0, 2))
-    grad_front, grad_gain_query, grad_gain_key = qk_pull(
-        (
-            query_grad.astype(F32).reshape(TOKENS, QUERY_HEADS, HEAD_SIZE),
-            key_value_grad[..., :HEAD_SIZE],
-        )
-    )
-    grad_values = key_value_grad[..., HEAD_SIZE:].reshape(TOKENS, KEY_VALUE_HEADS * HEAD_SIZE)
-    grad_projected = jnp.concatenate([grad_front, grad_values], axis=1).astype(BF16)
-    grad_normed = matmul(grad_projected, qkv_all.T)
-    grad_input_norm, grad_gain_attn = norm_in_pull(grad_normed)
-    grad_inputs = (grad_resid + grad_input_norm).astype(BF16)
+    grad_projected, grad_inputs, gains = project_back(
+        query_grad,
+        key_value_grad,
+        projected,
+        inputs[0],
+        grad_resid,
+        gain_row,
+        qkv_all,
+        *head_gains,
+        *tables,
+        grad_gain_ffn.reshape(1, D),
+    )
 
     (projected_pair,) = share([grad_projected], [], 9)
-    gains = jnp.concatenate([grad_gain_attn, grad_gain_ffn, grad_gain_query, grad_gain_key])
-    gains = jnp.pad(gains, (0, 24 * 128 - gains.shape[0])).reshape(24, 128)
     grad_qkv, grad_out_weight, grad_gate_weight, grad_up_weight, grad_down, gains = reduce_weights(
         nears, outer_sum(normed_half, projected_pair), gains
     )
@@ -1255,7 +1370,7 @@
         grad_down.astype(F32),
         gains[:D],
         gains[2 * D : 2 * D + HEAD_SIZE],
-        gains[2 * D + HEAD_SIZE : 2 * D + 2 * HEAD_SIZE],
+        gains[2 * D + 128 : 2 * D + 128 + HEAD_SIZE],
         gains[D : 2 * D],
     )
 

time: 422 us -> 365 us (0.86)
  local copies, waits for them, and re-layouts: 54.5 us -> 24.9 us
  other arithmetic: 33.7 us -> 18.4 us
  matrix products: 30 us -> 23.8 us
    pallas_call x11, Pallas kernels: 294 us -> 284 us  [wired_call(): pl.pallas_call(kernel, out_shape=outs, in_specs=[ANY] * len(ins) if in_sp...]
    unnamed x198 -> x120, local copies, waits for them, and re-layouts: 32.7 us -> 22.1 us
    slice x9 -> x1, local copies, waits for them, and re-layouts: 7.9 us -> 0.52 us  [per_device(): gains[2 * D + 128:2 * D + 128 + HEAD_SIZE]]
    reshape x6 -> x0, local copies, waits for them, and re-layouts: 6.68 us -> none  [the longest x1 2.04 us: query_key(): leading_columns[:, :QUERY_HEADS * HEAD_SIZE]]
    pallas_call x0 -> x2, Pallas kernels: none -> 6.66 us  [the longest x1 4.52 us: project_back(): pl.pallas_call(project_back_kernel, out_shape=[shape(TOKENS, 2048), shape...]
    dot_general x10 -> x8, matrix products: 16.9 us -> 10.8 us  [matmul(): return jnp.dot(left, right, preferred_element_type=F32)]
where the time goes in v1:
time: 365 us; the launch traced here: 359 us
  Pallas kernels  290 us (79%)
  local copies, waits for them, and re-layouts  24.9 us (7%)
  matrix products  23.8 us (7%)
  other arithmetic  18.4 us (5%)
    pallas_call x11, Pallas kernels, wired_call(): pl.pallas_call(kernel, out_shape=outs, in_specs=[ANY] * len(ins) if in_sp...  284 us
    unnamed x120, local copies, waits for them, and re-layouts  22.1 us
    dot_general x5, matrix products, outer_sum(): lax.dot_general(left, right, (((0,), (0,)), ((), ())), preferred_element_...  13 us
    dot_general x8, matrix products, matmul(): return jnp.dot(left, right, preferred_element_type=F32)  10.8 us

profile of v1, /device:TPU:0, one launch (start us, length us, event | category | flops | bytes accessed | tf_op | source)
XLA Modules:
  0.0 359.2 jit_solution(13394596670745416365)
XLA Ops:
  1.8 1.7 copy-done.14
  3.4 1.7 copy-done.15
  5.1 1.7 copy-done.16
  9.0 38.3 %gather.1 = (bf16[2,2,4,4,16,2048]{5,4,3,2,1,0:T(8,128)(2,1)S(1)}, bf16[2,2,4,4,16,1024]{5,4,3,2,1,0:T(8,128)(2,1)S(1)}, bf16[2,2,4,4,16,2304]{5,4,3,2,1,0:T(8,1...) custom-call(bf16[4,4,16,2048]{3,2,1,0:T(8,128)(2,1)S(1)} %bitcast.133, ...), custom_call_target="tpu_custom_call" | custom-call | tf_op jit(solution)/shard_map/gather/pallas_call | solution.py:106
  47.5 2.1 project.1
  50.6 20.7 %to_heads.1 = (bf16[8,128,128]{2,1,0:T(8,128)(2,1)S(1)}, bf16[32,128,128]{2,1,0:T(8,128)(2,1)S(1)}) custom-call(bf16[128,1024]{1,0:T(8,128)(2,1)S(1)} %get-tuple-element.60.query, bf16[128,1024]{1,0:T(8,128)(2,1)S(1)} %get-tuple-element.61.key_value), custom_call_target="tpu_custom_call" | custom-call | tf_op jit(solution)/shard_map/to_heads/pallas_call | solution.py:106
  71.4 31.0 %attend.1 = (bf16[16,64,128]{2,1,0:T(8,128)(2,1)S(1)}, f32[16,128,128]{2,1,0:T(8,128)S(1)}, f32[16,8,128]{2,1,0:T(8,128)S(1)}, bf16[2,2,4,4,16,2304]{5,4,3,2,1,0...) custom-call(s32[4]{0:T(128)S(1)} %bitcast.147, ...), custom_call_target="tpu_custom_call", output_to_operand_aliasing={{3}: (4, {}), {4}: (5, {}), {5}: (6, {})} | custom-call | tf_op jit(solution)/shard_map/attend/pallas_call | solution.py:106
  102.5 7.0 %to_tokens.1.refs_3_ = bf16[128,1024]{1,0:T(8,128)(2,1)S(1)} custom-call(bf16[8,128,128]{2,1,0:T(8,128)(2,1)S(1)} %bitcast.140), custom_call_target="tpu_custom_call" | custom-call | tf_op jit(solution)/shard_map/to_tokens/pallas_call | solution.py:106
  110.2 2.6 share.2
  115.8 2.4 multiply_convert_fusion
  118.2 1.4 fusion.25
  119.6 1.4 convolution_add_fusion
  121.1 1.4 fusion.24.refs_0_
  122.5 2.8 hand_over.1
  127.2 1.6 multiply_reduce_fusion
  129.4 1.9 fusion.15
  132.2 7.7 %grad_to_heads.1 = (bf16[8,128,128]{2,1,0:T(8,128)(2,1)S(1)}, bf16[2,128,1024]{2,1,0:T(8,128)(2,1)S(1)}) custom-call(bf16[128,1024]{1,0:T(8,128)(2,1)S(1)} %convolution_convert_fusion.3.grad, bf16[128,1024]{1,0:T(8,128)(2,1)S(1)} %get-tuple-element.109.branch), custom_call_target="tpu_custom_call" | custom-call | tf_op jit(solution)/shard_map/grad_to_heads/pallas_call | solution.py:106
  139.9 1.4 bitcast_convert_fusion.2
  141.3 3.6 %convolution_convert_fusion = bf16[2304,1024]{1,0:T(8,128)(2,1)} fusion(bf16[256,2304]{1,0:T(8,128)(2,1)S(1)} %copy-done.48, bf16[256,1024]{1,0:T(8,128)(2,1)S(1)} %bitcast.138), kind=kOutput, calls=%fused_computation | convolution fusion | flops 1210318848 | bytes 6422528 | tf_op jit(solution)/shard_map/dot_general | solution.py:1242
  144.9 3.6 %convolution_convert_fusion.1 = bf16[1024,2304]{1,0:T(8,128)(2,1)} fusion(bf16[256,1024]{1,0:T(8,128)(2,1)S(1)} %bitcast.116, bf16[256,2304]{1,0:T(8,128)(2,1)S(1)} %copy-done.52), kind=kOutput, calls=%fused_computation.1 | convolution fusion | flops 1210318848 | bytes 6422528 | tf_op jit(solution)/shard_map/dot_general | solution.py:1242
  148.5 3.6 %convolution_convert_fusion.2 = bf16[1024,2304]{1,0:T(8,128)(2,1)} fusion(bf16[256,1024]{1,0:T(8,128)(2,1)S(1)} %bitcast.117, bf16[256,2304]{1,0:T(8,128)(2,1)S(1)} %copy-done.50), kind=kOutput, calls=%fused_computation.2 | convolution fusion | flops 1210318848 | bytes 6422528 | tf_op jit(solution)/shard_map/dot_general | solution.py:1242
  152.2 76.4 %attend_back.1 = (bf16[16,64,128]{2,1,0:T(8,128)(2,1)}, bf16[4096,128]{1,0:T(8,128)(2,1)}, bf16[16,2304]{1,0:T(8,128)(2,1)}, bf16[16,2304]{1,0:T(8,128)(2,1)}, b...) custom-call(s32[4]{0:T(128)} %bitcast.146, s32[64]{0:T(128)} %refs_1_.1, bf16[16,64,128]{2,1,0:T(8,128)(2,1)} %bitcast.132, ...), custom_call_target="tpu_custom_call" | custom-call | tf_op jit(solution)/shard_map/attend_back/pallas_call | solution.py:106
  234.2 31.1 %grads_to_tokens.1 = (bf16[128,1024]{1,0:T(8,128)(2,1)S(1)}, bf16[32,128,128]{2,1,0:T(8,128)(2,1)S(1)}, bf16[2,4,4,16,2304]{4,3,2,1,0:T(8,128)(2,1)S(1)}, bf16[2...) custom-call(bf16[8,128,128]{2,1,0:T(8,128)(2,1)S(1)} %bitcast.141, ...), custom_call_target="tpu_custom_call" | custom-call | tf_op jit(solution)/shard_map/grads_to_tokens/pallas_call | solution.py:106
  267.8 4.5 %project_back.1 = (bf16[128,2048]{1,0:T(8,128)(2,1)S(1)}, bf16[128,1024]{1,0:T(8,128)(2,1)}, f32[24,128]{1,0:T(8,128)S(1)}) custom-call(bf16[128,1024]{1,0:T(8,128)(2,1)S(1)} %get-tuple-element.88.query_grad_ref, bf16[32,128,128]{2,1,0:T(8,128)(2,1)S(1)} %get-tuple-element.89.key_value_grad_ref, f32[128,1536]{1,0:T(8,128)S(1)} %copy-done.25, ...), custom_call_target="tpu_custom_call" | custom-call | tf_op jit(solution)/shard_map/project_back/pallas_call | solution.py:1217
  272.3 1.9 share.3
  275.9 64.1 %reduce_weights.1 = (bf16[2,4,4,16,2304]{4,3,2,1,0:T(8,128)(2,1)S(1)}, bf16[2,4,4,16,2304]{4,3,2,1,0:T(8,128)(2,1)S(1)}, bf16[4,2,144,1024]{3,2,1,0:T(8,128)(2,1...) custom-call(bf16[2,4,4,16,2304]{4,3,2,1,0:T(8,128)(2,1)S(1)} %get-tu, ...), custom_call_target="tpu_custom_call", output_to_operand_aliasing={{0}: (0, {}), {1}: (1, {}), {2}: (2, {}), {3}: (3, {})} | custom-call | tf_op jit(solution)/shard_map/reduce_weights/pallas_call | solution.py:106
  341.4 1.4 copy-done.4
  344.2 1.5 bitcast_select_fusion.1
  345.9 2.7 maximum_convert_fusion.1
  349.3 2.7 maximum_convert_fusion
  352.0 2.9 bitcast_convert_fusion.1
  354.9 1.6 bitcast_convert_fusion.3
  (141 shorter events, 26.7 us)
Async XLA Ops:
  9.0 38.3 %copy-start.55 = (f32[64]{0:T(128)S(1)}, f32[64]{0:T(128)}, u32[]{:S(2)}) copy-start(f32[64]{0:T(128)} %param.21) | copy-start | bytes 772
  9.0 38.3 %copy-start.56 = (f32[64]{0:T(128)S(1)}, f32[64]{0:T(128)}, u32[]{:S(2)}) copy-start(f32[64]{0:T(128)} %param.22) | copy-start | bytes 772
  9.0 38.4 %copy-start.13 = (bf16[1,128,1024]{2,1,0:T(8,128)(2,1)S(1)}, bf16[1,128,1024]{2,1,0:T(8,128)(2,1)}, u32[]{:S(2)}) copy-start(bf16[1,128,1024]{2,1,0:T(8,128)(2,1)} %param.13) | copy-start | bytes 786436
  9.0 38.4 %copy-start.42 = (f32[1024]{0:T(1024)S(1)}, f32[1024]{0:T(1024)}, u32[]{:S(2)}) copy-start(f32[1024]{0:T(1024)} %param.20) | copy-start | bytes 12292
  47.4 24.0 %copy-start = (bf16[2,2,4,4,16,2048]{5,4,3,2,1,0:T(8,128)(2,1)}, bf16[2,2,4,4,16,2048]{5,4,3,2,1,0:T(8,128)(2,1)S(1)}, u32[]{:S(2)}) copy-start(bf16[2,2,4,4,16,2048]{5,4,3,2,1,0:T(8,128)(2,1)S(1)} %get-tuple-element.59) | copy-start | bytes 12582916
  47.5 23.9 %copy-start.8 = (bf16[2,2,4,4,16,2304]{5,4,3,2,1,0:T(8,128)(2,1)S(1)}, bf16[2,2,4,4,16,2304]{5,4,3,2,1,0:T(8,128)(2,1)}, u32[]{:S(2)}) copy-start(bf16[2,2,4,4,16,2304]{5,4,3,2,1,0:T(8,128)(2,1)} %get-tuple-element.65.up_in) | copy-start | bytes 14155780
  47.5 23.9 %copy-start.43 = (s32[1,4]{1,0:T(1,128)S(1)}, s32[1,4]{1,0:T(1,128)}, u32[]{:S(2)}) copy-start(s32[1,4]{1,0:T(1,128)} %param.25) | copy-start | bytes 52
  47.5 23.9 %copy-start.44 = (s32[64]{0:T(128)S(1)}, s32[64]{0:T(128)}, u32[]{:S(2)}) copy-start(s32[64]{0:T(128)} %refs_1_.1) | copy-start | bytes 772
  71.3 31.1 %copy-start.9 = (bf16[32,128,128]{2,1,0:T(8,128)(2,1)}, bf16[32,128,128]{2,1,0:T(8,128)(2,1)S(1)}, u32[]{:S(2)}) copy-start(bf16[32,128,128]{2,1,0:T(8,128)(2,1)S(1)} %get-tuple-element.63) | copy-start | bytes 3145732
  71.3 31.1 %copy-start.17 = (bf16[8,128,128]{2,1,0:T(8,128)(2,1)}, bf16[8,128,128]{2,1,0:T(8,128)(2,1)S(1)}, u32[]{:S(2)}) copy-start(bf16[8,128,128]{2,1,0:T(8,128)(2,1)S(1)} %get-tuple-element.62) | copy-start | bytes 786436
  102.4 10.4 %copy-start.19 = (f32[16,128,128]{2,1,0:T(8,128)}, f32[16,128,128]{2,1,0:T(8,128)S(1)}, u32[]{:S(2)}) copy-start(f32[16,128,128]{2,1,0:T(8,128)S(1)} %get-tuple-element.78.refs_5_) | copy-start | bytes 3145732
  102.4 10.4 %copy-start.40 = (f32[16,8,128]{2,1,0:T(8,128)}, f32[16,8,128]{2,1,0:T(8,128)S(1)}, u32[]{:S(2)}) copy-start(f32[16,8,128]{2,1,0:T(8,128)S(1)} %get-tuple-element.79.refs_6_) | copy-start | bytes 196612
  102.5 7.6 %copy-start.53 = (f32[1024]{0:T(1024)S(1)}, f32[1024]{0:T(1024)}, u32[]{:S(2)}) copy-start(f32[1024]{0:T(1024)} %param.23) | copy-start | bytes 12292
  102.5 7.8 %copy-start.23 = (bf16[1,128,1024]{2,1,0:T(8,128)(2,1)S(1)}, bf16[1,128,1024]{2,1,0:T(8,128)(2,1)}, u32[]{:S(2)}) copy-start(bf16[1,128,1024]{2,1,0:T(8,128)(2,1)} %param.14) | copy-start | bytes 786436
  110.1 4.2 %copy-start.45 = (f32[128,1024]{1,0:T(8,128)}, f32[128,1024]{1,0:T(8,128)S(1)}, u32[]{:S(2)}) copy-start(f32[128,1024]{1,0:T(8,128)S(1)} %get-tuple-element.135) | copy-start | bytes 1572868
  110.1 4.2 %copy-start.57 = (f32[128]{0:T(128)}, f32[128]{0:T(128)S(1)}, u32[]{:S(2)}) copy-start(f32[128]{0:T(128)S(1)} %get-tuple-element.134) | copy-start | bytes 1540
  110.1 4.2 %copy-start.54 = (f32[128]{0:T(128)}, f32[128]{0:T(128)S(1)}, u32[]{:S(2)}) copy-start(f32[128]{0:T(128)S(1)} %fusion.14) | copy-start | bytes 1540
  112.9 2.9 copy-start.29
  112.9 2.9 slice-start
  118.2 2.9 copy-start.47
  127.2 2.2 copy-start.46
  131.3 8.5 %copy-start.35 = (bf16[2,128,512]{2,1,0:T(8,128)(2,1)S(1)}, bf16[2,128,512]{2,1,0:T(8,128)(2,1)}, u32[]{:S(2)}) copy-start(bf16[2,128,512]{2,1,0:T(8,128)(2,1)} %copy-done.34) | copy-start | bytes 786436
  131.3 10.0 %copy-start.30 = (bf16[2,128,1024]{2,1,0:T(8,128)(2,1)S(1)}, bf16[2,128,1024]{2,1,0:T(8,128)(2,1)}, u32[]{:S(2)}) copy-start(bf16[2,128,1024]{2,1,0:T(8,128)(2,1)} %copy-done.29) | copy-start | bytes 1572868
  131.3 10.0 %copy-start.48 = (bf16[256,2304]{1,0:T(8,128)(2,1)S(1)}, bf16[256,2304]{1,0:T(8,128)(2,1)}, u32[]{:S(2)}) copy-start(bf16[256,2304]{1,0:T(8,128)(2,1)} %copy-done.47) | copy-start | bytes 3538948
  139.8 5.1 %copy-start.33 = (bf16[8,128,128]{2,1,0:T(8,128)(2,1)}, bf16[8,128,128]{2,1,0:T(8,128)(2,1)S(1)}, u32[]{:S(2)}) copy-start(bf16[8,128,128]{2,1,0:T(8,128)(2,1)S(1)} %get-tuple-element.77) | copy-start | bytes 786436
  141.3 3.6 %copy-start.52 = (bf16[256,2304]{1,0:T(8,128)(2,1)S(1)}, bf16[256,2304]{1,0:T(8,128)(2,1)}, u32[]{:S(2)}) copy-start(bf16[256,2304]{1,0:T(8,128)(2,1)} %copy-done.51) | copy-start | bytes 3538948
  144.9 3.6 %copy-start.50 = (bf16[256,2304]{1,0:T(8,128)(2,1)S(1)}, bf16[256,2304]{1,0:T(8,128)(2,1)}, u32[]{:S(2)}) copy-start(bf16[256,2304]{1,0:T(8,128)(2,1)} %copy-done.49) | copy-start | bytes 3538948
  152.2 114.5 %copy-start.1 = (bf16[2,2,4,4,16,2048]{5,4,3,2,1,0:T(8,128)(2,1)S(1)}, bf16[2,2,4,4,16,2048]{5,4,3,2,1,0:T(8,128)(2,1)}, u32[]{:S(2)}) copy-start(bf16[2,2,4,4,16,2048]{5,4,3,2,1,0:T(8,128)(2,1)} %copy-done) | copy-start | bytes 12582916
  267.8 6.5 %copy-start.27 = (bf16[2,128,512]{2,1,0:T(8,128)(2,1)S(1)}, bf16[2,128,512]{2,1,0:T(8,128)(2,1)}, u32[]{:S(2)}) copy-start(bf16[2,128,512]{2,1,0:T(8,128)(2,1)} %copy-done.26) | copy-start | bytes 786436
  345.9 2.8 copy-start.5
  349.3 2.8 copy-start.3
  352.0 2.9 copy-start.21
  (28 other events, 37.1 us)

commit v2 on v1

--- a/solution.py
+++ b/solution.py
@@ -404,6 +404,7 @@
         7,
         in_specs=[HBM] * 5,
         out_specs=[ANY] * 2 + [HBM] * 3,
+        vmem=60 * MIB,
     )
     return qkv.reshape(D, 2048), out.reshape(D, D), wide
 
@@ -423,21 +424,16 @@
     (0, RowsByShard(HALF_FF), ("z", "x", "y"), ("y", "x", "z")),
     (1, RowsByShard(HALF_FF), ("x", "y", "z"), ("z", "y", "x")),
     (2, ColumnsByY(144), ("y", "z", "x"), ("x", "z", "y")),
-    (3, ColumnsByY(32), ("y", "z", "x"), ("x", "z", "y")),
 )
 NARROW = (
     (0, RowsByPlane(0, 1024), ("z", "x", "y"), ("z", "y", "x")),
     (0, RowsByPlane(1024, 1024), ("x", "y", "z"), ("x", "z", "y")),
+    (1, ColumnsByY(32), ("y", "z", "x"), ("z", "x", "y")),
 )
-FIRST_DIRECT = ("y", "y", "x", "x")
-WIDE_DIMS = (
-    (2, 2, 4, 4, 16, HALF_FF),
-    (2, 2, 4, 4, 16, HALF_FF),
-    (2, 4, 2, 144, D),
-    (2, 4, 2, 32, D),
-)
-QKV_DIMS = (2, 4, 4, 16, 2048)
-PIECE_DIMS = ((16, HALF_FF), (16, HALF_FF), (144, 256), (32, 256))
+FIRST_DIRECT = ("y", "y", "x")
+WIDE_DIMS = ((2, 2, 4, 4, 16, HALF_FF), (2, 2, 4, 4, 16, HALF_FF), (2, 4, 2, 144, D))
+NARROW_DIMS = ((2, 4, 4, 16, 2048), (2, 4, 2, 32, D))
+PIECE_DIMS = ((16, HALF_FF), (16, HALF_FF), (144, 256))
 
 
 def slot_shapes(parts):
@@ -542,11 +538,10 @@
 
 
 def reduce_weights_kernel(*refs):
-    grad, gains = refs[4:6]
-    nears, (gate_beside, up_beside, qkv_out, gains_out) = (refs[6:10], refs[10:14])
-    total, slots = (refs[14], refs[15:21])
-    gain_slots, sends, receives, moves = refs[21:]
-    besides = (gate_beside, up_beside)
+    grads, gains = (refs[3:5], refs[5])
+    nears, boths, narrow_outs, gains_out = (refs[6:9], refs[9:11], refs[11:13], refs[13])
+    totals, slots = (refs[14:16], refs[16:25])
+    gain_slots, sends, receives, moves = refs[25:]
 
     here = Place()
     wires = Wires(sends, receives, moves)
@@ -574,13 +569,14 @@
         gains_out[...] = sums
 
     def narrow(p):
-        _, kind, order, back = NARROW[p]
+        g, kind, order, back = NARROW[p]
         yield from reduce_one(
-            here, wires, kind, grad, total, slots[3 * p : 3 * p + 3], order, 1
+            here, wires, kind, grads[g], totals[g], slots[3 * p : 3 * p + 3], order, 1
         )
-        own = wires.move(kind.view(total, held), kind.view(qkv_out, held, 1))
+        out = narrow_outs[g]
+        own = wires.move(kind.view(totals[g], held), kind.view(out, held, 1))
         own.wait()
-        yield from spread(here, wires, kind, qkv_out, held, back, 1, direct="xy")
+        yield from spread(here, wires, kind, out, held, back, 1, direct="xy")
 
     def wide(p):
         _, kind, _, back = WIDE[p]
@@ -589,58 +585,59 @@
             at = without(at, axis)
         yield from spread(here, wires, kind, nears[p], at, back[2:], 1)
         if p < 2:
-            copies = [wires.push(nears[p].at[1 - core], besides[p], sibling)]
+            copies = [wires.push(nears[p].at[1 - core], boths[p].at[core], sibling)]
+            own = wires.move(nears[p].at[core], boths[p].at[core])
             yield
             arrive(copies)
+            own.wait()
 
     in_turn(
-        [narrow(p) for p in range(2)]
-        + [later(wide(p), rounds) for p, rounds in ((1, 2), (2, 2), (3, 1), (0, 4))]
+        [narrow(p) for p in range(3)]
+        + [later(wide(p), rounds) for p, rounds in ((1, 2), (2, 2), (0, 4))]
         + [all_gains()]
     )
     wires.finish_sends()
 
 
-def reduce_weights(nears, qkv, gains):
+def reduce_weights(nears, qkv, out, gains):
     outs = [
         *(shape(*d[1:]) for d in WIDE_DIMS),
-        shape(*WIDE_DIMS[0][2:]),
-        shape(*WIDE_DIMS[1][2:]),
-        shape(*QKV_DIMS[1:]),
+        shape(*WIDE_DIMS[0][1:]),
+        shape(*WIDE_DIMS[1][1:]),
+        *(shape(*d[1:]) for d in NARROW_DIMS),
         shape(*gains.shape, dtype=F32),
     ]
-    scratch = [pltpu.VMEM(QKV_DIMS, BF16)]
+    scratch = [pltpu.VMEM(d, BF16) for d in NARROW_DIMS]
     scratch += [pltpu.VMEM(s, BF16) for s in slot_shapes(NARROW)]
     scratch += [pltpu.VMEM((4, 4, *gains.shape), F32)]
-    gate, up, down, out, gate_beside, up_beside, qkv, gains = wired_call(
+    narrow = [a.reshape(d) for a, d in zip((qkv, out), NARROW_DIMS)]
+    _, _, down, gate, up, qkv, out, gains = wired_call(
         reduce_weights_kernel,
         outs,
-        [*nears, qkv.reshape(QKV_DIMS), gains],
+        [*nears, *narrow, gains],
         2,
         "reduce_weights",
-        10 + 2 * (18 + 7) + 1 + 3 * 4 + 2,
-        2 * 4,
+        10 + 3 * (18 + 7) + 1 + 2 * 4 + 2,
+        3 * 4 + 2,
         scratch,
-        [HBM] * 4 + [ANY] + [VMEM],
+        [HBM] * 3 + [ANY] * 2 + [VMEM],
         [HBM] * 7 + [VMEM],
-        vmem=40 * MIB,
-        aliases={i: i for i in range(4)},
-    )
-    core = lax.axis_index("fsdp") % 2
-
-    def joined(near, beside):
-        own = lax.dynamic_index_in_dim(near, core, 0, keepdims=False).reshape(256, HALF_FF)
-        beside = beside.reshape(256, HALF_FF)
-        first, second = (jnp.where(core == 0, own, beside), jnp.where(core == 0, beside, own))
-        pieces = [f[:, r * SLICE : (r + 1) * SLICE] for r in range(2) for f in (first, second)]
+        vmem=60 * MIB,
+        aliases={i: i for i in range(3)},
+    )
+
+    def joined(both):
+        both = both.reshape(2, 256, HALF_FF)
+        pieces = [
+            both[c, :, r * SLICE : (r + 1) * SLICE] for r in range(2) for c in range(2)
+        ]
         return jnp.concatenate(pieces, axis=1)
 
-    gate, up = (joined(gate, gate_beside), joined(up, up_beside))
     return (
         qkv.reshape(256, 2048),
         out.reshape(256, D),
-        gate,
-        up,
+        joined(gate),
+        joined(up),
         down.reshape(SLICE, D),
         gains,
     )
@@ -729,10 +726,10 @@
 
 
 def grads_to_tokens_kernel(*refs):
-    query, key_value, pieces = (refs[0], refs[1], refs[2:6])
-    query_out, key_value_out, nears = (refs[6], refs[7], refs[8:12])
+    query, key_value, pieces = (refs[0], refs[1], refs[2:5])
+    query_out, key_value_out, nears = (refs[5], refs[6], refs[7:10])
     here = Place()
-    wires = Wires(*refs[12:])
+    wires = Wires(*refs[10:])
     me, seat, near, far = seats(here)
     greet([(k, here.fsdp) for k in far])
     held = {"zh": here.zh, "zl": here.zl, "x": here.x, "y": here.y}
@@ -761,7 +758,7 @@
             here, wires, kind, nears[p], held, order[:2], 1, direct=FIRST_DIRECT[p]
         )
 
-    in_turn([share(p) for p in range(4)] + [back()])
+    in_turn([share(p) for p in range(3)] + [back()])
     wires.finish_sends()
 
 
@@ -772,10 +769,11 @@
         [query, key_value, *pieces],
         6,
         "grads_to_tokens",
-        38 + 7 + 4 + 4 + 4,
-        6,
-        in_specs=[ANY] * 2 + [HBM] * 4,
-        out_specs=[ANY] * 2 + [HBM] * 4,
+        38 + 7 + 4 + 4,
+        5,
+        in_specs=[ANY] * 2 + [HBM] * 3,
+        out_specs=[ANY] * 2 + [HBM] * 3,
+        vmem=60 * MIB,
     )
     return query_grad, key_value_grad, nears
 
@@ -1049,11 +1047,11 @@
 
 
 def attend_back_kernel(*refs):
-    attention, grads = (refs[:7], refs[7:11])
-    outs, pieces = (refs[11:13], refs[13:17])
-    scratch, totals, slots = (refs[17:20], refs[20:24], refs[24:36])
+    attention, grads = (refs[:7], refs[7:10])
+    outs, pieces = (refs[10:12], refs[12:15])
+    scratch, totals, slots = (refs[15:18], refs[18:21], refs[21:30])
     here = Place()
-    wires = Wires(*refs[36:])
+    wires = Wires(*refs[30:])
     greet_rings(here)
     at = {"zh": here.zh, "zl": here.zl, "x": here.x, "y": here.y}
 
@@ -1068,7 +1066,7 @@
 
     first_block = here.ctx // QUARTER * 16
     in_turn(
-        [reduce(p) for p in range(4)]
+        [reduce(p) for p in range(3)]
         + [attend_back_task((3, 3, 1, 1), first_block, *attention, *outs, *scratch)]
     )
     wires.finish_sends()
@@ -1090,11 +1088,11 @@
         ins,
         11,
         "attend_back",
-        4 * 18,
-        4 * 4,
+        3 * 18,
+        3 * 4,
         scratch,
-        [SMEM] * 2 + [VMEM] * 5 + [HBM] * 4,
-        [VMEM] * 2 + [HBM] * 4,
+        [SMEM] * 2 + [VMEM] * 5 + [HBM] * 3,
+        [VMEM] * 2 + [HBM] * 3,
         vmem=58 * MIB,
     )
     return query_grad, key_value_grad, pieces
@@ -1334,7 +1332,6 @@
             outer_sum(ffn_pair, gate_low),
             outer_sum(ffn_pair, up_low),
             outer_sum(hidden_low, cotangent_pair),
-            outer_sum(attended_half, branch_pair.reshape(2 * TOKENS, D)),
         ),
     )
     query_grad, key_value_grad, nears = grads_to_tokens(
@@ -1357,7 +1354,10 @@
 
     (projected_pair,) = share([grad_projected], [], 9)
     grad_qkv, grad_out_weight, grad_gate_weight, grad_up_weight, grad_down, gains = reduce_weights(
-        nears, outer_sum(normed_half, projected_pair), gains
+        nears,
+        outer_sum(normed_half, projected_pair),
+        outer_sum(attended_half, branch_pair.reshape(2 * TOKENS, D)),
+        gains,
     )
     gains = gains.reshape(-1)
     return (

time: 365 us -> 577 us (1.58)
  Pallas kernels: 290 us -> 522 us
  local copies, waits for them, and re-layouts: 24.9 us -> 12.3 us
    pallas_call x11, Pallas kernels: 284 us -> 515 us  [wired_call(): pl.pallas_call(kernel, out_shape=outs, in_specs=[ANY] * len(ins) if in_sp...]
    unnamed x120 -> x50, local copies, waits for them, and re-layouts: 22.1 us -> 9.4 us
where the time goes in v2:
time: 577 us; the launch traced here: 576 us
  Pallas kernels  522 us (90%)
  matrix products  25.5 us (4%)
  other arithmetic  15.6 us (3%)
  local copies, waits for them, and re-layouts  12.3 us (2%)
    pallas_call x11, Pallas kernels, wired_call(): pl.pallas_call(kernel, out_shape=outs, in_specs=[ANY] * len(ins) if in_sp...  515 us
    dot_general x5, matrix products, outer_sum(): lax.dot_general(left, right, (((0,), (0,)), ((), ())), preferred_element_...  14.5 us

profile of v2, /device:TPU:0, one launch (start us, length us, event | category | flops | bytes accessed | tf_op | source)
XLA Modules:
  0.0 576.5 jit_solution(7127998176717698710)
XLA Ops:
  2.6 197.1 %gather.1 = (bf16[2,2,4,4,16,2048]{5,4,3,2,1,0:T(8,128)(2,1)}, bf16[2,2,4,4,16,1024]{5,4,3,2,1,0:T(8,128)(2,1)}, bf16[2,2,4,4,16,2304]{5,4,3,2,1,0:T(8,128)(2,1)...) custom-call(bf16[4,4,16,2048]{3,2,1,0:T(8,128)(2,1)} %bitcast.160, ...), custom_call_target="tpu_custom_call" | custom-call | tf_op jit(solution)/shard_map/gather/pallas_call | solution.py:106
  199.8 2.2 copy-done
  201.9 2.2 project.1
  204.1 24.0 %to_heads.1 = (bf16[8,128,128]{2,1,0:T(8,128)(2,1)S(1)}, bf16[32,128,128]{2,1,0:T(8,128)(2,1)S(1)}) custom-call(bf16[128,1024]{1,0:T(8,128)(2,1)S(1)} %get-tuple-element.56.query, bf16[128,1024]{1,0:T(8,128)(2,1)S(1)} %get-tuple-element.57.key_value), custom_call_target="tpu_custom_call" | custom-call | tf_op jit(solution)/shard_map/to_heads/pallas_call | solution.py:106
  228.2 2.8 copy-done.3
  231.0 30.2 %attend.1 = (bf16[16,64,128]{2,1,0:T(8,128)(2,1)S(1)}, f32[16,128,128]{2,1,0:T(8,128)S(1)}, f32[16,8,128]{2,1,0:T(8,128)S(1)}, bf16[2,2,4,4,16,2304]{5,4,3,2,1,0...) custom-call(s32[4]{0:T(128)S(1)} %bitcast.142, ...), custom_call_target="tpu_custom_call", output_to_operand_aliasing={{3}: (4, {}), {4}: (5, {}), {5}: (6, {})} | custom-call | tf_op jit(solution)/shard_map/attend/pallas_call | solution.py:106
  261.2 7.0 %to_tokens.1.refs_3_ = bf16[128,1024]{1,0:T(8,128)(2,1)S(1)} custom-call(bf16[8,128,128]{2,1,0:T(8,128)(2,1)S(1)} %bitcast.137), custom_call_target="tpu_custom_call" | custom-call | tf_op jit(solution)/shard_map/to_tokens/pallas_call | solution.py:106
  269.0 2.6 share.2
  271.6 1.4 fusion.19
  273.0 1.4 fusion.18
  274.5 2.6 multiply_convert_fusion
  277.1 1.4 fusion.21
  278.5 1.4 convolution_add_fusion
  279.9 1.5 fusion.20.refs_0_
  281.4 2.8 hand_over.1
  286.2 7.7 %grad_to_heads.1 = (bf16[8,128,128]{2,1,0:T(8,128)(2,1)S(1)}, bf16[2,128,1024]{2,1,0:T(8,128)(2,1)S(1)}) custom-call(bf16[128,1024]{1,0:T(8,128)(2,1)S(1)} %convolution_convert_fusion.3.grad, bf16[128,1024]{1,0:T(8,128)(2,1)S(1)} %get-tuple-element.101.branch), custom_call_target="tpu_custom_call" | custom-call | tf_op jit(solution)/shard_map/grad_to_heads/pallas_call | solution.py:106
  293.9 1.5 bitcast_convert_fusion.2
  295.4 3.6 convolution_convert_fusion.1
  299.0 3.6 convolution_convert_fusion.2
  302.7 3.6 convolution_convert_fusion
  306.3 67.4 %attend_back.1 = (bf16[16,64,128]{2,1,0:T(8,128)(2,1)}, bf16[4096,128]{1,0:T(8,128)(2,1)}, bf16[16,2304]{1,0:T(8,128)(2,1)}, bf16[16,2304]{1,0:T(8,128)(2,1)}, bf16[144,256]{1,0:T(8,128)(2,1)}) custom-call(s32[4]{0:T(128)} %bitcast.141, s32[64]{0:T(128)} %refs_1_.1, bf16[16,64,128]{2,1,0:T(8,128)(2,1)} %bitcast.132, bf16[4096,128]{1,0:T(8,128)(2,1)} %bitcast.126, ...), custom_call_target="tpu_custom_call" | custom-call | tf_op jit(solution)/shard_map/attend_back/pallas_call | solution.py:106
  373.6 43.7 %grads_to_tokens.1 = (bf16[128,1024]{1,0:T(8,128)(2,1)}, bf16[32,128,128]{2,1,0:T(8,128)(2,1)}, bf16[2,4,4,16,2304]{4,3,2,1,0:T(8,128)(2,1)}, bf16[2,4,4,16,2304...) custom-call(bf16[8,128,128]{2,1,0:T(8,128)(2,1)} %bitcast.163, bf16[32,128,128]{2,1,0:T(8,128)(2,1)} %bitcast.161, ...), custom_call_target="tpu_custom_call" | custom-call | tf_op jit(solution)/shard_map/grads_to_tokens/pallas_call | solution.py:106
  417.3 2.2 copy-done.1
  421.7 4.6 project_back.1
  426.3 1.9 share.3
  428.2 2.1 bitcast_convert_fusion
  430.3 130.8 %reduce_weights.1 = (bf16[2,4,4,16,2304]{4,3,2,1,0:T(8,128)(2,1)}, bf16[2,4,4,16,2304]{4,3,2,1,0:T(8,128)(2,1)}, bf16[4,2,144,1024]{3,2,1,0:T(8,128)(2,1)}, bf16...) custom-call(bf16[2,4,4,16,2304]{4,3,2,1,0:T(8,128)(2,1)} %get-tuple-, ...), custom_call_target="tpu_custom_call", output_to_operand_aliasing={{0}: (0, {}), {1}: (1, {}), {2}: (2, {})} | custom-call | tf_op jit(solution)/shard_map/reduce_weights/pallas_call | solution.py:106
  561.1 1.3 fusion.17
  563.6 2.9 bitcast_convert_fusion.3
  567.9 2.7 maximum_convert_fusion
  570.8 2.7 maximum_convert_fusion.1
  573.6 2.9 bitcast_convert_fusion.1
  (65 shorter events, 9.6 us)
Async XLA Ops:
  2.6 197.1 %copy-start.5 = (bf16[1,128,1024]{2,1,0:T(8,128)(2,1)S(1)}, bf16[1,128,1024]{2,1,0:T(8,128)(2,1)}, u32[]{:S(2)}) copy-start(bf16[1,128,1024]{2,1,0:T(8,128)(2,1)} %param.13) | copy-start | bytes 786436
  2.6 197.1 %copy-start.13 = (f32[1024]{0:T(1024)S(1)}, f32[1024]{0:T(1024)}, u32[]{:S(2)}) copy-start(f32[1024]{0:T(1024)} %param.20) | copy-start | bytes 12292
  199.7 2.2 copy-start
  201.9 26.2 %copy-start.2 = (bf16[2,2,4,4,16,2304]{5,4,3,2,1,0:T(8,128)(2,1)S(1)}, bf16[2,2,4,4,16,2304]{5,4,3,2,1,0:T(8,128)(2,1)}, u32[]{:S(2)}) copy-start(bf16[2,2,4,4,16,2304]{5,4,3,2,1,0:T(8,128)(2,1)} %get-tuple-element.60.gate_in) | copy-start | bytes 14155780
  201.9 26.2 %copy-start.15 = (s32[1,4]{1,0:T(1,128)S(1)}, s32[1,4]{1,0:T(1,128)}, u32[]{:S(2)}) copy-start(s32[1,4]{1,0:T(1,128)} %param.25) | copy-start | bytes 52
  201.9 26.2 %copy-start.16 = (s32[64]{0:T(128)S(1)}, s32[64]{0:T(128)}, u32[]{:S(2)}) copy-start(s32[64]{0:T(128)} %refs_1_.1) | copy-start | bytes 772
  228.1 33.0 %copy-start.4 = (bf16[32,128,128]{2,1,0:T(8,128)(2,1)}, bf16[32,128,128]{2,1,0:T(8,128)(2,1)S(1)}, u32[]{:S(2)}) copy-start(bf16[32,128,128]{2,1,0:T(8,128)(2,1)S(1)} %get-tuple-element.59) | copy-start | bytes 3145732
  228.1 33.0 %copy-start.6 = (bf16[8,128,128]{2,1,0:T(8,128)(2,1)}, bf16[8,128,128]{2,1,0:T(8,128)(2,1)S(1)}, u32[]{:S(2)}) copy-start(bf16[8,128,128]{2,1,0:T(8,128)(2,1)S(1)} %get-tuple-element.58) | copy-start | bytes 786436
  228.2 2.8 copy-start.3
  231.0 37.3 %copy-start.18 = (bf16[2,2,4,4,16,1024]{5,4,3,2,1,0:T(8,128)(2,1)S(1)}, bf16[2,2,4,4,16,1024]{5,4,3,2,1,0:T(8,128)(2,1)}, u32[]{:S(2)}) copy-start(bf16[2,2,4,4,16,1024]{5,4,3,2,1,0:T(8,128)(2,1)} %get-tuple-element.64) | copy-start | bytes 6291460
  261.2 10.4 %copy-start.7 = (f32[16,128,128]{2,1,0:T(8,128)}, f32[16,128,128]{2,1,0:T(8,128)S(1)}, u32[]{:S(2)}) copy-start(f32[16,128,128]{2,1,0:T(8,128)S(1)} %get-tuple-element.74.refs_5_) | copy-start | bytes 3145732
  261.2 10.4 %copy-start.12 = (f32[16,8,128]{2,1,0:T(8,128)}, f32[16,8,128]{2,1,0:T(8,128)S(1)}, u32[]{:S(2)}) copy-start(f32[16,8,128]{2,1,0:T(8,128)S(1)} %get-tuple-element.75.refs_6_) | copy-start | bytes 196612
  261.2 7.6 %copy-start.22 = (f32[1024]{0:T(1024)S(1)}, f32[1024]{0:T(1024)}, u32[]{:S(2)}) copy-start(f32[1024]{0:T(1024)} %param.23) | copy-start | bytes 12292
  261.2 7.7 %copy-start.9 = (bf16[1,128,1024]{2,1,0:T(8,128)(2,1)S(1)}, bf16[1,128,1024]{2,1,0:T(8,128)(2,1)}, u32[]{:S(2)}) copy-start(bf16[1,128,1024]{2,1,0:T(8,128)(2,1)} %param.14) | copy-start | bytes 786436
  271.6 2.9 slice-start
  273.0 1.5 slice-start.1
  293.9 5.2 copy-start.10
  417.3 2.2 copy-start.1
  419.5 1.2 copy-start.8
  420.7 0.9 copy-start.11
  426.3 4.0 copy-start.14
  561.0 5.5 copy-start.21
  563.6 4.1 copy-start.20
  567.9 2.8 copy-start.19
  570.8 2.8 copy-start.17

commit v3 on v2

--- a/solution.py
+++ b/solution.py
@@ -326,22 +326,26 @@
         crossed = [self.wires.push(source, target, self.cross[0])]
         yield from self.rest(ColumnsByY(144), whole, crossed, order, "x")
 
-    def from_this_chip(self, narrow=(), wide=(), down=()):
+    def from_this_chip(self, shards, staged, wholes):
+        landed = [self.wires.move(shard, stage) for shard, stage in zip(shards, staged)]
+        yield
         beside, kept = ([], [])
-        for shard, whole in narrow:
-            target = whole.at[self.zh, self.core]
-            beside.append(self.wires.push(shard, target, self.sibling))
-            kept.append(self.wires.move(shard, target))
-        for shard, whole in wide:
-            for r in range(2):
-                target = whole.at[self.zh, self.core, :, :, :, pl.ds(r * SLICE, SLICE)]
-                theirs = shard.at[:, :, :, self.ff_columns(r, 1 - self.core)]
-                mine = shard.at[:, :, :, self.ff_columns(r, self.core)]
-                beside.append(self.wires.push(theirs, target, self.sibling))
-                kept.append(self.wires.move(mine, target))
-        for shard, whole in down:
-            kept.append(self.wires.move(shard, whole.at[self.zh]))
-        for _ in range(6):
+        for n, (stage, whole) in enumerate(zip(staged, wholes)):
+            landed[n].wait()
+            if n < 2:
+                target = whole.at[self.zh, self.core]
+                beside.append(self.wires.push(stage, target, self.sibling))
+                kept.append(self.wires.move(stage, target))
+            elif n < 4:
+                for r in range(2):
+                    target = whole.at[self.zh, self.core, :, :, :, pl.ds(r * SLICE, SLICE)]
+                    theirs = stage.at[:, :, :, self.ff_columns(r, 1 - self.core)]
+                    mine = stage.at[:, :, :, self.ff_columns(r, self.core)]
+                    beside.append(self.wires.push(theirs, target, self.sibling))
+                    kept.append(self.wires.move(mine, target))
+            else:
+                kept.append(self.wires.move(stage, whole.at[self.zh]))
+        for _ in range(4):
             yield
         arrive(beside)
         for copy in kept:
@@ -356,8 +360,9 @@
 
 
 def gather_kernel(
-    qkv, out, gate, up, down, qkv_all, out_all, gate_all, up_all, down_all, sends, receives, moves
+    qkv, out, gate, up, down, qkv_all, out_all, gate_all, up_all, down_all, *scratch
 ):
+    staged, (sends, receives, moves) = (scratch[:5], scratch[5:])
     wires = Wires(sends, receives, moves)
     here = Place()
     fetch = Fetch(here, wires)
@@ -371,9 +376,7 @@
             fetch.wide(up, up_all, WIDE_FETCH[1][1][:2]),
             fetch.down(down, down_all, WIDE_FETCH[2][1][:2]),
             fetch.from_this_chip(
-                ((qkv, qkv_all), (out, out_all)),
-                ((gate, gate_all), (up, up_all)),
-                ((down, down_all),),
+                (qkv, out, gate, up, down), staged, (qkv_all, out_all, gate_all, up_all, down_all)
             ),
         ]
     )
@@ -401,7 +404,14 @@
         1,
         "gather",
         3 * 8 + 9 + 6 + 5 + 6,
-        7,
+        12,
+        [
+            pltpu.VMEM((*rows, 2048), BF16),
+            pltpu.VMEM((*rows, D), BF16),
+            pltpu.VMEM((*rows, FF), BF16),
+            pltpu.VMEM((*rows, FF), BF16),
+            pltpu.VMEM((4, 2, 144, D), BF16),
+        ],
         in_specs=[HBM] * 5,
         out_specs=[ANY] * 2 + [HBM] * 3,
         vmem=60 * MIB,
@@ -433,7 +443,6 @@
 FIRST_DIRECT = ("y", "y", "x")
 WIDE_DIMS = ((2, 2, 4, 4, 16, HALF_FF), (2, 2, 4, 4, 16, HALF_FF), (2, 4, 2, 144, D))
 NARROW_DIMS = ((2, 4, 4, 16, 2048), (2, 4, 2, 32, D))
-PIECE_DIMS = ((16, HALF_FF), (16, HALF_FF), (144, 256))
 
 
 def slot_shapes(parts):
@@ -540,8 +549,8 @@
 def reduce_weights_kernel(*refs):
     grads, gains = (refs[3:5], refs[5])
     nears, boths, narrow_outs, gains_out = (refs[6:9], refs[9:11], refs[11:13], refs[13])
-    totals, slots = (refs[14:16], refs[16:25])
-    gain_slots, sends, receives, moves = refs[25:]
+    totals, slots, staged = (refs[14:16], refs[16:25], refs[25:27])
+    gain_slots, sends, receives, moves = refs[27:]
 
     here = Place()
     wires = Wires(sends, receives, moves)
@@ -586,7 +595,8 @@
         yield from spread(here, wires, kind, nears[p], at, back[2:], 1)
         if p < 2:
             copies = [wires.push(nears[p].at[1 - core], boths[p].at[core], sibling)]
-            own = wires.move(nears[p].at[core], boths[p].at[core])
+            wires.move(nears[p].at[core], staged[p]).wait()
+            own = wires.move(staged[p], boths[p].at[core])
             yield
             arrive(copies)
             own.wait()
@@ -609,6 +619,7 @@
     ]
     scratch = [pltpu.VMEM(d, BF16) for d in NARROW_DIMS]
     scratch += [pltpu.VMEM(s, BF16) for s in slot_shapes(NARROW)]
+    scratch += [pltpu.VMEM(WIDE_DIMS[0][2:], BF16)] * 2
     scratch += [pltpu.VMEM((4, 4, *gains.shape), F32)]
     narrow = [a.reshape(d) for a, d in zip((qkv, out), NARROW_DIMS)]
     _, _, down, gate, up, qkv, out, gains = wired_call(
@@ -618,7 +629,7 @@
         2,
         "reduce_weights",
         10 + 3 * (18 + 7) + 1 + 2 * 4 + 2,
-        3 * 4 + 2,
+        3 * 4 + 4,
         scratch,
         [HBM] * 3 + [ANY] * 2 + [VMEM],
         [HBM] * 7 + [VMEM],
@@ -726,23 +737,29 @@
 
 
 def grads_to_tokens_kernel(*refs):
-    query, key_value, pieces = (refs[0], refs[1], refs[2:5])
-    query_out, key_value_out, nears = (refs[5], refs[6], refs[7:10])
+    query, key_value = refs[:2]
+    query_out, key_value_out, nears, staged = (refs[5], refs[6], refs[7:10], refs[10:12])
     here = Place()
-    wires = Wires(*refs[10:])
+    wires = Wires(*refs[12:])
     me, seat, near, far = seats(here)
     greet([(k, here.fsdp) for k in far])
     held = {"zh": here.zh, "zl": here.zl, "x": here.x, "y": here.y}
 
     def back():
         columns = query_out.at[:, head_columns(seat)]
+        landed = [
+            wires.move(query.at[seat], staged[0]),
+            wires.move(key_value.at[me], staged[1]),
+        ]
         copies = [wires.push(query.at[k % QUARTER], columns, (k, here.fsdp)) for k in near]
         copies += [
             wires.push(key_value.at[k], key_value_out.at[me], (k, here.fsdp)) for k in far
         ]
+        for copy in landed:
+            copy.wait()
         kept = [
-            wires.move(query.at[seat], columns),
-            wires.move(key_value.at[me], key_value_out.at[me]),
+            wires.move(staged[0], columns),
+            wires.move(staged[1], key_value_out.at[me]),
         ]
         for _ in range(3):
             yield
@@ -752,8 +769,6 @@
 
     def share(p):
         _, kind, _, order = WIDE[p]
-        own = wires.move(pieces[p], kind.view(nears[p], held, 1))
-        own.wait()
         yield from spread(
             here, wires, kind, nears[p], held, order[:2], 1, direct=FIRST_DIRECT[p]
         )
@@ -762,18 +777,20 @@
     wires.finish_sends()
 
 
-def grads_to_tokens(query, key_value, pieces):
+def grads_to_tokens(query, key_value, nears):
     query_grad, key_value_grad, *nears = wired_call(
         grads_to_tokens_kernel,
         [shape(TOKENS, D), shape(RING, TOKENS, 128), *(shape(*d[1:]) for d in WIDE_DIMS)],
-        [query, key_value, *pieces],
+        [query, key_value, *nears],
         6,
         "grads_to_tokens",
         38 + 7 + 4 + 4,
-        5,
+        4,
+        [pltpu.VMEM((TOKENS, 128), BF16), pltpu.VMEM((TOKENS, 128), BF16)],
         in_specs=[ANY] * 2 + [HBM] * 3,
         out_specs=[ANY] * 2 + [HBM] * 3,
         vmem=60 * MIB,
+        aliases={2 + i: 2 + i for i in range(3)},
     )
     return query_grad, key_value_grad, nears
 
@@ -1048,7 +1065,7 @@
 
 def attend_back_kernel(*refs):
     attention, grads = (refs[:7], refs[7:10])
-    outs, pieces = (refs[10:12], refs[12:15])
+    outs, nears = (refs[10:12], refs[12:15])
     scratch, totals, slots = (refs[15:18], refs[18:21], refs[21:30])
     here = Place()
     wires = Wires(*refs[30:])
@@ -1060,7 +1077,7 @@
         yield from reduce_one(
             here, wires, kind, grads[p], totals[p], slots[3 * p : 3 * p + 3], order, 2
         )
-        own = wires.move(kind.view(totals[p], at), pieces[p])
+        own = wires.move(kind.view(totals[p], at), kind.view(nears[p], at, 1))
         yield
         own.wait()
 
@@ -1082,9 +1099,9 @@
     ]
     scratch += [pltpu.VMEM(d, BF16) for d in WIDE_DIMS]
     scratch += [pltpu.VMEM(s, BF16) for s in slot_shapes(WIDE)]
-    query_grad, key_value_grad, *pieces = wired_call(
+    query_grad, key_value_grad, *nears = wired_call(
         attend_back_kernel,
-        [shape(16, 64, 128), shape(SEQ, 128), *(shape(*d) for d in PIECE_DIMS)],
+        [shape(16, 64, 128), shape(SEQ, 128), *(shape(*d[1:]) for d in WIDE_DIMS)],
         ins,
         11,
         "attend_back",
@@ -1095,7 +1112,7 @@
         [VMEM] * 2 + [HBM] * 3,
         vmem=58 * MIB,
     )
-    return query_grad, key_value_grad, pieces
+    return query_grad, key_value_grad, nears
 
 
 def low_lanes():
@@ -1321,7 +1338,7 @@
     branch_low = grad_resid.astype(BF16)
     grad_attended = matmul(branch_low, out_all.T).astype(BF16)
     grad_part, branch_pair = grad_to_heads(grad_attended, branch_low)
-    query_grad, key_value_grad, pieces = attend_back(
+    query_grad, key_value_grad, nears = attend_back(
         *places,
         query_part,
         key_value_part,
@@ -1337,7 +1354,7 @@
     query_grad, key_value_grad, nears = grads_to_tokens(
         query_grad.reshape(QUARTER, TOKENS, 128),
         key_value_grad.reshape(RING, TOKENS, 128),
-        pieces,
+        nears,
     )
     grad_projected, grad_inputs, gains = project_back(
         query_grad,

time: 577 us -> 351 us (0.61)
  Pallas kernels: 522 us -> 296 us
    pallas_call x11, Pallas kernels: 515 us -> 289 us  [wired_call(): pl.pallas_call(kernel, out_shape=outs, in_specs=[ANY] * len(ins) if in_sp...]
where the time goes in v3:
time: 351 us
  Pallas kernels  296 us (84%)
  matrix products  25.6 us (7%)
  other arithmetic  15.6 us (4%)
  local copies, waits for them, and re-layouts  12.3 us (4%)
    pallas_call x11, Pallas kernels, wired_call(): pl.pallas_call(kernel, out_shape=outs, in_specs=[ANY] * len(ins) if in_sp...  289 us
    dot_general x5, matrix products, outer_sum(): lax.dot_general(left, right, (((0,), (0,)), ((), ())), preferred_element_...  14.5 us
    dot_general x8, matrix products, matmul(): return jnp.dot(left, right, preferred_element_type=F32)  11.1 us
    unnamed x50, local copies, waits for them, and re-layouts  9.4 us

profile of v3, /device:TPU:0, one launch (start us, length us, event | category | flops | bytes accessed | tf_op | source)
XLA Modules:
  0.0 350.5 jit_solution(5203051208339023299)
XLA Ops:
  2.6 39.0 %gather.1 = (bf16[2,2,4,4,16,2048]{5,4,3,2,1,0:T(8,128)(2,1)}, bf16[2,2,4,4,16,1024]{5,4,3,2,1,0:T(8,128)(2,1)}, bf16[2,2,4,4,16,2304]{5,4,3,2,1,0:T(8,128)(2,1)...) custom-call(bf16[4,4,16,2048]{3,2,1,0:T(8,128)(2,1)} %bitcast.160, ...), custom_call_target="tpu_custom_call" | custom-call | tf_op jit(solution)/shard_map/gather/pallas_call | solution.py:106
  41.7 2.2 copy-done
  43.8 2.2 project.1
  46.0 20.8 %to_heads.1 = (bf16[8,128,128]{2,1,0:T(8,128)(2,1)S(1)}, bf16[32,128,128]{2,1,0:T(8,128)(2,1)S(1)}) custom-call(bf16[128,1024]{1,0:T(8,128)(2,1)S(1)} %get-tuple-element.56.query, bf16[128,1024]{1,0:T(8,128)(2,1)S(1)} %get-tuple-element.57.key_value), custom_call_target="tpu_custom_call" | custom-call | tf_op jit(solution)/shard_map/to_heads/pallas_call | solution.py:106
  66.9 2.8 copy-done.3
  69.7 31.2 %attend.1 = (bf16[16,64,128]{2,1,0:T(8,128)(2,1)S(1)}, f32[16,128,128]{2,1,0:T(8,128)S(1)}, f32[16,8,128]{2,1,0:T(8,128)S(1)}, bf16[2,2,4,4,16,2304]{5,4,3,2,1,0...) custom-call(s32[4]{0:T(128)S(1)} %bitcast.142, ...), custom_call_target="tpu_custom_call", output_to_operand_aliasing={{3}: (4, {}), {4}: (5, {}), {5}: (6, {})} | custom-call | tf_op jit(solution)/shard_map/attend/pallas_call | solution.py:106
  101.0 7.0 %to_tokens.1.refs_3_ = bf16[128,1024]{1,0:T(8,128)(2,1)S(1)} custom-call(bf16[8,128,128]{2,1,0:T(8,128)(2,1)S(1)} %bitcast.137), custom_call_target="tpu_custom_call" | custom-call | tf_op jit(solution)/shard_map/to_tokens/pallas_call | solution.py:106
  108.7 2.6 share.2
  111.3 1.4 fusion.19
  112.8 1.4 fusion.18
  114.3 2.6 multiply_convert_fusion
  116.9 1.4 fusion.21
  118.3 1.4 convolution_add_fusion
  119.7 1.5 fusion.20.refs_0_
  121.2 2.8 hand_over.1
  126.0 7.7 %grad_to_heads.1 = (bf16[8,128,128]{2,1,0:T(8,128)(2,1)S(1)}, bf16[2,128,1024]{2,1,0:T(8,128)(2,1)S(1)}) custom-call(bf16[128,1024]{1,0:T(8,128)(2,1)S(1)} %convolution_convert_fusion.3.grad, bf16[128,1024]{1,0:T(8,128)(2,1)S(1)} %get-tuple-element.101.branch), custom_call_target="tpu_custom_call" | custom-call | tf_op jit(solution)/shard_map/grad_to_heads/pallas_call | solution.py:106
  133.7 1.5 bitcast_convert_fusion.2
  135.2 3.6 %convolution_convert_fusion.1 = bf16[1024,2304]{1,0:T(8,128)(2,1)} fusion(bf16[256,1024]{1,0:T(8,128)(2,1)S(1)} %bitcast.119, bf16[256,2304]{1,0:T(8,128)(2,1)S(1)} %get-tuple-element.104), kind=kOutput, calls=%fused_computation.1 | convolution fusion | flops 1210318848 | bytes 6422528 | tf_op jit(solution)/shard_map/dot_general | solution.py:1257
  138.8 3.6 %convolution_convert_fusion.2 = bf16[1024,2304]{1,0:T(8,128)(2,1)} fusion(bf16[256,1024]{1,0:T(8,128)(2,1)S(1)} %bitcast.120, bf16[256,2304]{1,0:T(8,128)(2,1)S(1)} %get-tuple-element.105), kind=kOutput, calls=%fused_computation.2 | convolution fusion | flops 1210318848 | bytes 6422528 | tf_op jit(solution)/shard_map/dot_general | solution.py:1257
  142.4 3.6 %convolution_convert_fusion = bf16[2304,1024]{1,0:T(8,128)(2,1)} fusion(bf16[256,2304]{1,0:T(8,128)(2,1)S(1)} %get-tuple-element.106, bf16[256,1024]{1,0:T(8,128)(2,1)S(1)} %bitcast.135), kind=kOutput, calls=%fused_computation | convolution fusion | flops 1210318848 | bytes 6422528 | tf_op jit(solution)/shard_map/dot_general | solution.py:1257
  146.1 66.8 %attend_back.1 = (bf16[16,64,128]{2,1,0:T(8,128)(2,1)}, bf16[4096,128]{1,0:T(8,128)(2,1)}, bf16[2,4,4,16,2304]{4,3,2,1,0:T(8,128)(2,1)}, bf16[2,4,4,16,2304]{4,3,2,1,0:T(8,128)(2,1)}, bf16[4,2,144,1024]{3,2,1,0:T(8,128)(2,1)}) custom-call(s32[4]{0:T(128)} %bitcast.141, s32[64]{0:T(128)} %refs_1_.1, bf16[16,64,128]{2,1,0:T(8,128)(2,1)} %bitcast.132, ...), custom_call_target="tpu_custom_call" | custom-call | tf_op jit(solution)/shard_map/attend_back/pallas_call | solution.py:106
  212.9 33.5 %grads_to_tokens.1 = (bf16[128,1024]{1,0:T(8,128)(2,1)}, bf16[32,128,128]{2,1,0:T(8,128)(2,1)}, bf16[2,4,4,16,2304]{4,3,2,1,0:T(8,128)(2,1)}, bf16[2,4,4,16,2304...) custom-call(bf16[8,128,128]{2,1,0:T(8,128)(2,1)} %bitcast.163, ...), custom_call_target="tpu_custom_call", output_to_operand_aliasing={{2}: (2, {}), {3}: (3, {}), {4}: (4, {})} | custom-call | tf_op jit(solution)/shard_map/grads_to_tokens/pallas_call | solution.py:106
  246.4 2.2 copy-done.1
  250.8 4.6 %project_back.1 = (bf16[128,2048]{1,0:T(8,128)(2,1)S(1)}, bf16[128,1024]{1,0:T(8,128)(2,1)}, f32[24,128]{1,0:T(8,128)S(1)}) custom-call(bf16[128,1024]{1,0:T(8,128)(2,1)S(1)} %copy-done.11, bf16[32,128,128]{2,1,0:T(8,128)(2,1)S(1)} %copy-done.8, f32[128,1536]{1,0:T(8,128)S(1)} %get-tuple-element.83.projected_ref, bf16[128,1024]{1,0:T(8,128)(2,1)S(1)} %bitcast.130, ...), custom_call_target="tpu_custom_call" | custom-call | tf_op jit(solution)/shard_map/project_back/pallas_call | solution.py:1232
  255.3 1.9 share.3
  257.3 2.1 bitcast_convert_fusion
  259.4 75.7 %reduce_weights.1 = (bf16[2,4,4,16,2304]{4,3,2,1,0:T(8,128)(2,1)}, bf16[2,4,4,16,2304]{4,3,2,1,0:T(8,128)(2,1)}, bf16[4,2,144,1024]{3,2,1,0:T(8,128)(2,1)}, bf16...) custom-call(bf16[2,4,4,16,2304]{4,3,2,1,0:T(8,128)(2,1)} %get-tuple-, ...), custom_call_target="tpu_custom_call", output_to_operand_aliasing={{0}: (0, {}), {1}: (1, {}), {2}: (2, {})} | custom-call | tf_op jit(solution)/shard_map/reduce_weights/pallas_call | solution.py:106
  335.1 1.3 fusion.17
  337.7 2.9 bitcast_convert_fusion.3
  342.0 2.7 maximum_convert_fusion
  344.9 2.7 maximum_convert_fusion.1
  347.7 2.9 bitcast_convert_fusion.1
  (65 shorter events, 9.6 us)
Async XLA Ops:
  2.6 39.1 %copy-start.5 = (bf16[1,128,1024]{2,1,0:T(8,128)(2,1)S(1)}, bf16[1,128,1024]{2,1,0:T(8,128)(2,1)}, u32[]{:S(2)}) copy-start(bf16[1,128,1024]{2,1,0:T(8,128)(2,1)} %param.13) | copy-start | bytes 786436
  2.6 39.1 %copy-start.13 = (f32[1024]{0:T(1024)S(1)}, f32[1024]{0:T(1024)}, u32[]{:S(2)}) copy-start(f32[1024]{0:T(1024)} %param.20) | copy-start | bytes 12292
  41.7 2.2 copy-start
  43.8 23.1 %copy-start.2 = (bf16[2,2,4,4,16,2304]{5,4,3,2,1,0:T(8,128)(2,1)S(1)}, bf16[2,2,4,4,16,2304]{5,4,3,2,1,0:T(8,128)(2,1)}, u32[]{:S(2)}) copy-start(bf16[2,2,4,4,16,2304]{5,4,3,2,1,0:T(8,128)(2,1)} %get-tuple-element.60.gate_in) | copy-start | bytes 14155780
  43.8 23.1 %copy-start.15 = (s32[1,4]{1,0:T(1,128)S(1)}, s32[1,4]{1,0:T(1,128)}, u32[]{:S(2)}) copy-start(s32[1,4]{1,0:T(1,128)} %param.25) | copy-start | bytes 52
  43.8 23.1 %copy-start.16 = (s32[64]{0:T(128)S(1)}, s32[64]{0:T(128)}, u32[]{:S(2)}) copy-start(s32[64]{0:T(128)} %refs_1_.1) | copy-start | bytes 772
  66.9 34.1 %copy-start.4 = (bf16[32,128,128]{2,1,0:T(8,128)(2,1)}, bf16[32,128,128]{2,1,0:T(8,128)(2,1)S(1)}, u32[]{:S(2)}) copy-start(bf16[32,128,128]{2,1,0:T(8,128)(2,1)S(1)} %get-tuple-element.59) | copy-start | bytes 3145732
  66.9 34.1 %copy-start.6 = (bf16[8,128,128]{2,1,0:T(8,128)(2,1)}, bf16[8,128,128]{2,1,0:T(8,128)(2,1)S(1)}, u32[]{:S(2)}) copy-start(bf16[8,128,128]{2,1,0:T(8,128)(2,1)S(1)} %get-tuple-element.58) | copy-start | bytes 786436
  66.9 2.8 copy-start.3
  69.7 38.3 %copy-start.18 = (bf16[2,2,4,4,16,1024]{5,4,3,2,1,0:T(8,128)(2,1)S(1)}, bf16[2,2,4,4,16,1024]{5,4,3,2,1,0:T(8,128)(2,1)}, u32[]{:S(2)}) copy-start(bf16[2,2,4,4,16,1024]{5,4,3,2,1,0:T(8,128)(2,1)} %get-tuple-element.64) | copy-start | bytes 6291460
  100.9 10.4 %copy-start.7 = (f32[16,128,128]{2,1,0:T(8,128)}, f32[16,128,128]{2,1,0:T(8,128)S(1)}, u32[]{:S(2)}) copy-start(f32[16,128,128]{2,1,0:T(8,128)S(1)} %get-tuple-element.74.refs_5_) | copy-start | bytes 3145732
  101.0 10.4 %copy-start.12 = (f32[16,8,128]{2,1,0:T(8,128)}, f32[16,8,128]{2,1,0:T(8,128)S(1)}, u32[]{:S(2)}) copy-start(f32[16,8,128]{2,1,0:T(8,128)S(1)} %get-tuple-element.75.refs_6_) | copy-start | bytes 196612
  101.0 7.6 %copy-start.22 = (f32[1024]{0:T(1024)S(1)}, f32[1024]{0:T(1024)}, u32[]{:S(2)}) copy-start(f32[1024]{0:T(1024)} %param.23) | copy-start | bytes 12292
  101.0 7.7 %copy-start.9 = (bf16[1,128,1024]{2,1,0:T(8,128)(2,1)S(1)}, bf16[1,128,1024]{2,1,0:T(8,128)(2,1)}, u32[]{:S(2)}) copy-start(bf16[1,128,1024]{2,1,0:T(8,128)(2,1)} %param.14) | copy-start | bytes 786436
  111.3 2.9 slice-start
  112.8 1.5 slice-start.1
  133.7 5.2 %copy-start.10 = (bf16[8,128,128]{2,1,0:T(8,128)(2,1)}, bf16[8,128,128]{2,1,0:T(8,128)(2,1)S(1)}, u32[]{:S(2)}) copy-start(bf16[8,128,128]{2,1,0:T(8,128)(2,1)S(1)} %get-tuple-element.73) | copy-start | bytes 786436
  246.4 2.2 copy-start.1
  248.6 1.2 copy-start.8
  249.8 0.9 copy-start.11
  255.3 4.0 %copy-start.14 = (f32[24,128]{1,0:T(8,128)}, f32[24,128]{1,0:T(8,128)S(1)}, u32[]{:S(2)}) copy-start(f32[24,128]{1,0:T(8,128)S(1)} %get-tuple-element.92.refs_5_) | copy-start | bytes 36868
  335.1 5.5 %copy-start.21 = (bf16[4,2,32,1024]{3,2,1,0:T(8,128)(2,1)S(1)}, bf16[4,2,32,1024]{3,2,1,0:T(8,128)(2,1)}, u32[]{:S(2)}) copy-start(bf16[4,2,32,1024]{3,2,1,0:T(8,128)(2,1)} %get-tuple-element.94) | copy-start | bytes 1572868
  337.7 4.1 %copy-start.20 = (bf16[2,4,4,16,2304]{4,3,2,1,0:T(8,128)(2,1)S(1)}, bf16[2,4,4,16,2304]{4,3,2,1,0:T(8,128)(2,1)}, u32[]{:S(2)}) copy-start(bf16[2,4,4,16,2304]{4,3,2,1,0:T(8,128)(2,1)} %get-tuple-element.95) | copy-start | bytes 7077892
  341.9 2.8 copy-start.19
  344.9 2.8 copy-start.17

commit v4 on v3

--- a/solution.py
+++ b/solution.py
@@ -235,6 +235,12 @@
 def later(task, rounds):
     next(task)
     for _ in range(rounds + 1):
+        yield
+    yield from task
+
+
+def delayed(task, rounds):
+    for _ in range(rounds):
         yield
     yield from task
 
@@ -587,26 +593,70 @@
         own.wait()
         yield from spread(here, wires, kind, out, held, back, 1, direct="xy")
 
-    def wide(p):
+    def wide(p, c):
         _, kind, _, back = WIDE[p]
-        at = held
-        for axis in back[:2]:
-            at = without(at, axis)
-        yield from spread(here, wires, kind, nears[p], at, back[2:], 1)
+        axis = back[2]
+        cut = "y" if axis == "x" else "x"
+        at = {"zh": here.zh, cut: c}
+        if axis == "z":
+            at["zl"] = here.zl
+        else:
+            at[axis] = getattr(here, axis)
+        yield from spread(here, wires, kind, nears[p], at, (axis,), 1)
         if p < 2:
-            copies = [wires.push(nears[p].at[1 - core], boths[p].at[core], sibling)]
-            wires.move(nears[p].at[core], staged[p]).wait()
-            own = wires.move(staged[p], boths[p].at[core])
+            part = (c,) if cut == "x" else (slice(None), c)
+            mine = (core, *part)
+            copies = [wires.push(nears[p].at[(1 - core, *part)], boths[p].at[mine], sibling)]
+            wires.move(nears[p].at[mine], staged[p].at[part]).wait()
+            own = wires.move(staged[p].at[part], boths[p].at[mine])
             yield
             arrive(copies)
             own.wait()
 
     in_turn(
         [narrow(p) for p in range(3)]
-        + [later(wide(p), rounds) for p, rounds in ((1, 2), (2, 2), (0, 4))]
+        + [delayed(later(wide(p, c), 1), c) for c in range(4) for p in (1, 2, 0)]
         + [all_gains()]
     )
     wires.finish_sends()
+
+
+def widen_kernel(qkv, out, gate, up, down, qkv_out, out_out, gate_out, up_out, down_out):
+    qkv_out[...] = qkv[...].astype(F32)
+    out_out[...] = out[...].astype(F32)
+    down_out[...] = down[...].astype(F32)
+    for both, whole in ((gate, gate_out), (up, up_out)):
+        for r in range(2):
+            for c in range(2):
+                first = r * HALF_FF + c * SLICE
+                values = both[c, :, r * SLICE : (r + 1) * SLICE]
+                whole[:, first : first + SLICE] = values.astype(F32)
+
+
+def widen(qkv, out, gate, up, down):
+    steps = 8
+
+    def rows(n, columns):
+        return pl.BlockSpec((n // steps, columns), lambda i: (i, 0))
+
+    pair = pl.BlockSpec((2, 256 // steps, HALF_FF), lambda i: (0, i, 0))
+    return pl.pallas_call(
+        widen_kernel,
+        grid=(steps,),
+        out_shape=[
+            shape(256, 2048, dtype=F32),
+            shape(256, D, dtype=F32),
+            shape(256, FF, dtype=F32),
+            shape(256, FF, dtype=F32),
+            shape(SLICE, D, dtype=F32),
+        ],
+        in_specs=[rows(256, 2048), rows(256, D), pair, pair, rows(SLICE, D)],
+        out_specs=[
+            rows(256, 2048), rows(256, D), rows(256, FF), rows(256, FF), rows(SLICE, D)
+        ],
+        compiler_params=pltpu.CompilerParams(vmem_limit_bytes=60 * MIB),
+        name="widen",
+    )(qkv, out, gate, up, down)
 
 
 def reduce_weights(nears, qkv, out, gains):
@@ -628,8 +678,8 @@
         [*nears, *narrow, gains],
         2,
         "reduce_weights",
-        10 + 3 * (18 + 7) + 1 + 2 * 4 + 2,
-        3 * 4 + 4,
+        10 + 3 * (18 + 7) + 4 * (1 + 2 * 4 + 2),
+        3 * 4 + 4 * 4,
         scratch,
         [HBM] * 3 + [ANY] * 2 + [VMEM],
         [HBM] * 7 + [VMEM],
@@ -637,21 +687,14 @@
         aliases={i: i for i in range(3)},
     )
 
-    def joined(both):
-        both = both.reshape(2, 256, HALF_FF)
-        pieces = [
-            both[c, :, r * SLICE : (r + 1) * SLICE] for r in range(2) for c in range(2)
-        ]
-        return jnp.concatenate(pieces, axis=1)
-
-    return (
+    widened = widen(
         qkv.reshape(256, 2048),
         out.reshape(256, D),
-        joined(gate),
-        joined(up),
+        gate.reshape(2, 256, HALF_FF),
+        up.reshape(2, 256, HALF_FF),
         down.reshape(SLICE, D),
-        gains,
-    )
+    )
+    return (*widened, gains)
 
 
 def head_columns(head):
@@ -983,7 +1026,7 @@
         [pltpu.VMEM((SEQ, 128), BF16), pltpu.VMEM((1, SEQ), jnp.int32)],
         [SMEM] * 2 + [VMEM] * 2 + [HBM] * 3,
         [VMEM] * 3 + [HBM] * 3,
-        vmem=40 * MIB,
+        vmem=60 * MIB,
         aliases={4 + i: 3 + i for i in range(3)},
     )
     weights = (gate.reshape(D, HALF_FF), up.reshape(D, HALF_FF), down.reshape(HALF_FF, D))
@@ -1136,12 +1179,15 @@
 
 
 def project_kernel(
-    x_ref, gain_ref, weight_ref, query_gain_ref, key_gain_ref, cosine_ref, sine_ref, normed_ref,
-    query_ref, key_value_ref, projected_ref,
+    x_ref, gain_ref, weight_hbm, query_gain_ref, key_gain_ref, cosine_ref, sine_ref, normed_ref,
+    query_ref, key_value_ref, projected_ref, weight_ref, weight_sem,
 ):
+    fetch = pltpu.make_async_copy(weight_hbm, weight_ref, weight_sem)
+    fetch.start()
     x = x_ref[...].astype(F32)
     normed = x * lax.rsqrt(jnp.mean(x * x, axis=-1, keepdims=True) + EPSILON) * gain_ref[...]
     normed_ref[...] = normed.astype(BF16)
+    fetch.wait()
     projected = nn(normed_ref[...], weight_ref[...])
     projected_ref[...] = projected[:, :1536]
     low = low_lanes()
@@ -1171,18 +1217,21 @@
             shape(TOKENS, D),
             shape(TOKENS, 1536, dtype=F32),
         ],
-        in_specs=[VMEM] * 7,
+        in_specs=[VMEM] * 2 + [ANY] + [VMEM] * 4,
         out_specs=[VMEM] * 4,
-        compiler_params=pltpu.CompilerParams(vmem_limit_bytes=32 * MIB),
+        scratch_shapes=[pltpu.VMEM((D, 2048), BF16), pltpu.SemaphoreType.DMA],
+        compiler_params=pltpu.CompilerParams(vmem_limit_bytes=60 * MIB),
         name="project",
     )(x, gain, weight, query_gain, key_gain, cosine, sine)
 
 
 def project_back_kernel(
-    query_grad_ref, key_value_grad_ref, projected_ref, x_ref, grad_resid_ref, gain_ref, weight_ref,
+    query_grad_ref, key_value_grad_ref, projected_ref, x_ref, grad_resid_ref, gain_ref, weight_hbm,
     query_gain_ref, key_gain_ref, cosine_ref, sine_ref, ffn_gain_grad_ref, grad_projected_ref,
-    grad_inputs_ref, gains_ref,
+    grad_inputs_ref, gains_ref, weight_ref, weight_sem,
 ):
+    fetch = pltpu.make_async_copy(weight_hbm, weight_ref, weight_sem)
+    fetch.start()
     low = low_lanes()
 
     def back(j, grad, gain):
@@ -1211,6 +1260,7 @@
         key_gain_grad += back(8 + j, keys, key_gain_ref[...])
         grad_projected_ref[:, chunk(12 + j)] = values.astype(BF16)
 
+    fetch.wait()
     grad = nt(grad_projected_ref[...], weight_ref[...])
     x = x_ref[...].astype(F32)
     scale = lax.rsqrt(jnp.mean(x * x, axis=-1, keepdims=True) + EPSILON)
@@ -1232,9 +1282,10 @@
     return pl.pallas_call(
         project_back_kernel,
         out_shape=[shape(TOKENS, 2048), shape(TOKENS, D), shape(24, 128, dtype=F32)],
-        in_specs=[VMEM] * 12,
+        in_specs=[VMEM] * 6 + [ANY] + [VMEM] * 5,
         out_specs=[VMEM] * 3,
-        compiler_params=pltpu.CompilerParams(vmem_limit_bytes=40 * MIB),
+        scratch_shapes=[pltpu.VMEM((D, 2048), BF16), pltpu.SemaphoreType.DMA],
+        compiler_params=pltpu.CompilerParams(vmem_limit_bytes=60 * MIB),
         name="project_back",
     )(*ins)
 
@@ -1380,11 +1431,11 @@
     return (
         outputs.astype(BF16)[None],
         grad_inputs[None],
-        grad_qkv.astype(F32),
-        grad_out_weight.astype(F32),
-        grad_gate_weight.astype(F32),
-        grad_up_weight.astype(F32),
-        grad_down.astype(F32),
+        grad_qkv,
+        grad_out_weight,
+        grad_gate_weight,
+        grad_up_weight,
+        grad_down,
         gains[:D],
         gains[2 * D : 2 * D + HEAD_SIZE],
         gains[2 * D + 128 : 2 * D + 128 + HEAD_SIZE],

time: 351 us -> 343 us (0.977)
  other arithmetic: 15.6 us -> 5.05 us
  Pallas kernels: 296 us -> 303 us
  local copies, waits for them, and re-layouts: 12.3 us -> 8.2 us
    convert_element_type x5 -> x0, other arithmetic: 12.4 us -> none  [the longest x1 2.94 us: per_device(): grad_qkv.astype(F32)]
    pallas_call x0 -> x1, Pallas kernels: none -> 10.2 us  [widen(): pl.pallas_call(widen_kernel, grid=(steps,), out_shape=[shape(256, 2048, d...]
    pallas_call x11, Pallas kernels: 289 us -> 280 us  [wired_call(): pl.pallas_call(kernel, out_shape=outs, in_specs=[ANY] * len(ins) if in_sp...]
    pallas_call x1, Pallas kernels: 2.17 us -> 5.97 us  [project(): pl.pallas_call(project_kernel, out_shape=[shape(TOKENS, D), shape(TOKENS,...]
    unnamed x50 -> x34, local copies, waits for them, and re-layouts: 9.4 us -> 5.64 us
where the time goes in v4:
time: 343 us; the launch traced here: 342 us
  Pallas kernels  303 us (88%)
  matrix products  25.3 us (7%)
  local copies, waits for them, and re-layouts  8.2 us (2%)
  other arithmetic  5.05 us (1%)
    pallas_call x11, Pallas kernels, wired_call(): pl.pallas_call(kernel, out_shape=outs, in_specs=[ANY] * len(ins) if in_sp...  280 us
    dot_general x5, matrix products, outer_sum(): lax.dot_general(left, right, (((0,), (0,)), ((), ())), preferred_element_...  14.4 us
    dot_general x8, matrix products, matmul(): return jnp.dot(left, right, preferred_element_type=F32)  10.8 us
    pallas_call x1, Pallas kernels, widen(): pl.pallas_call(widen_kernel, grid=(steps,), out_shape=[shape(256, 2048, d...  10.2 us

profile of v4, /device:TPU:0, one launch (start us, length us, event | category | flops | bytes accessed | tf_op | source)
XLA Modules:
  0.0 342.4 jit_solution(12402955767507504891)
XLA Ops:
  1.4 1.3 maximum_bitcast_fusion
  2.8 1.0 fusion.8
  3.8 38.8 %gather.1 = (bf16[2,2,4,4,16,2048]{5,4,3,2,1,0:T(8,128)(2,1)}, bf16[2,2,4,4,16,1024]{5,4,3,2,1,0:T(8,128)(2,1)}, bf16[2,2,4,4,16,2304]{5,4,3,2,1,0:T(8,128)(2,1)...) custom-call(bf16[4,4,16,2048]{3,2,1,0:T(8,128)(2,1)} %bitcast.136, ...), custom_call_target="tpu_custom_call" | custom-call | tf_op jit(solution)/shard_map/gather/pallas_call | solution.py:106
  42.6 6.0 %project.1 = (bf16[128,1024]{1,0:T(8,128)(2,1)}, bf16[128,1024]{1,0:T(8,128)(2,1)}, bf16[128,1024]{1,0:T(8,128)(2,1)}, f32[128,1536]{1,0:T(8,128)}) custom-call(bf16[128,1024]{1,0:T(8,128)(2,1)} %bitcast.129, f32[1,1024]{1,0:T(1,128)} %bitcast.143, bf16[1024,2048]{1,0:T(8,128)(2,1)} %bitcast.112, f32[1,128]{1,0:T(1,128)} %get-tuple-element.128.query_gain_ref, ...), custom_call_target="tpu_custom_call" | custom-call | tf_op jit(solution)/shard_map/project/pallas_call | solution.py:1212
  50.5 20.6 %to_heads.1 = (bf16[8,128,128]{2,1,0:T(8,128)(2,1)S(1)}, bf16[32,128,128]{2,1,0:T(8,128)(2,1)S(1)}) custom-call(bf16[128,1024]{1,0:T(8,128)(2,1)S(1)} %copy-done.6, bf16[128,1024]{1,0:T(8,128)(2,1)S(1)} %copy-done.7), custom_call_target="tpu_custom_call" | custom-call | tf_op jit(solution)/shard_map/to_heads/pallas_call | solution.py:106
  72.8 33.5 %attend.1 = (bf16[16,64,128]{2,1,0:T(8,128)(2,1)}, f32[16,128,128]{2,1,0:T(8,128)}, f32[16,8,128]{2,1,0:T(8,128)}, bf16[2,2,4,4,16,2304]{5,4,3,2,1,0:T(8,128)(2,...) custom-call(s32[4]{0:T(128)} %bitcast.146, ...), custom_call_target="tpu_custom_call", output_to_operand_aliasing={{3}: (4, {}), {4}: (5, {}), {5}: (6, {})} | custom-call | tf_op jit(solution)/shard_map/attend/pallas_call | solution.py:106
  106.3 1.0 copy-done.5
  107.3 6.9 %to_tokens.1.refs_3_ = bf16[128,1024]{1,0:T(8,128)(2,1)S(1)} custom-call(bf16[8,128,128]{2,1,0:T(8,128)(2,1)S(1)} %bitcast.107), custom_call_target="tpu_custom_call" | custom-call | tf_op jit(solution)/shard_map/to_tokens/pallas_call | solution.py:106
  114.9 2.6 share.2
  117.5 1.4 fusion.19
  118.9 1.4 fusion.18
  120.4 2.5 multiply_convert_fusion
  122.9 1.4 fusion.21
  124.3 1.4 convolution_add_fusion
  125.7 1.4 fusion.20.refs_0_
  127.1 2.8 hand_over.1
  130.7 1.1 fusion.15
  132.6 7.7 %grad_to_heads.1 = (bf16[8,128,128]{2,1,0:T(8,128)(2,1)S(1)}, bf16[2,128,1024]{2,1,0:T(8,128)(2,1)S(1)}) custom-call(bf16[128,1024]{1,0:T(8,128)(2,1)S(1)} %convolution_convert_fusion.3.grad, bf16[128,1024]{1,0:T(8,128)(2,1)S(1)} %get-tuple-element.111.branch), custom_call_target="tpu_custom_call" | custom-call | tf_op jit(solution)/shard_map/grad_to_heads/pallas_call | solution.py:106
  140.3 1.5 bitcast_convert_fusion.1
  141.8 3.6 %convolution_convert_fusion.1 = bf16[1024,2304]{1,0:T(8,128)(2,1)} fusion(bf16[256,1024]{1,0:T(8,128)(2,1)S(1)} %bitcast.95, bf16[256,2304]{1,0:T(8,128)(2,1)S(1)} %get-tuple-element.114), kind=kOutput, calls=%fused_computation.1 | convolution fusion | flops 1210318848 | bytes 6422528 | tf_op jit(solution)/shard_map/dot_general | solution.py:1308
  145.4 3.6 %convolution_convert_fusion.2 = bf16[1024,2304]{1,0:T(8,128)(2,1)} fusion(bf16[256,1024]{1,0:T(8,128)(2,1)S(1)} %bitcast.96, bf16[256,2304]{1,0:T(8,128)(2,1)S(1)} %get-tuple-element.115), kind=kOutput, calls=%fused_computation.2 | convolution fusion | flops 1210318848 | bytes 6422528 | tf_op jit(solution)/shard_map/dot_general | solution.py:1308
  149.0 3.6 %convolution_convert_fusion = bf16[2304,1024]{1,0:T(8,128)(2,1)} fusion(bf16[256,2304]{1,0:T(8,128)(2,1)S(1)} %get-tuple-element.116, bf16[256,1024]{1,0:T(8,128)(2,1)S(1)} %bitcast.105), kind=kOutput, calls=%fused_computation | convolution fusion | flops 1210318848 | bytes 6422528 | tf_op jit(solution)/shard_map/dot_general | solution.py:1308
  152.6 66.9 %attend_back.1 = (bf16[16,64,128]{2,1,0:T(8,128)(2,1)}, bf16[4096,128]{1,0:T(8,128)(2,1)}, bf16[2,4,4,16,2304]{4,3,2,1,0:T(8,128)(2,1)}, bf16[2,4,4,16,2304]{4,3,2,1,0:T(8,128)(2,1)}, bf16[4,2,144,1024]{3,2,1,0:T(8,128)(2,1)}) custom-call(s32[4]{0:T(128)} %bitcast.147, s32[64]{0:T(128)} %refs_1_.1, bf16[16,64,128]{2,1,0:T(8,128)(2,1)} %bitcast.102, ...), custom_call_target="tpu_custom_call" | custom-call | tf_op jit(solution)/shard_map/attend_back/pallas_call | solution.py:106
  219.5 33.7 %grads_to_tokens.1 = (bf16[128,1024]{1,0:T(8,128)(2,1)}, bf16[32,128,128]{2,1,0:T(8,128)(2,1)}, bf16[2,4,4,16,2304]{4,3,2,1,0:T(8,128)(2,1)}, bf16[2,4,4,16,2304...) custom-call(bf16[8,128,128]{2,1,0:T(8,128)(2,1)} %bitcast.141, ...), custom_call_target="tpu_custom_call", output_to_operand_aliasing={{2}: (2, {}), {3}: (3, {}), {4}: (4, {})} | custom-call | tf_op jit(solution)/shard_map/grads_to_tokens/pallas_call | solution.py:106
  253.2 6.9 %project_back.1 = (bf16[128,2048]{1,0:T(8,128)(2,1)}, bf16[128,1024]{1,0:T(8,128)(2,1)}, f32[24,128]{1,0:T(8,128)}) custom-call(bf16[128,1024]{1,0:T(8,128)(2,1)} %get-tuple-element.86.query_grad_ref, bf16[32,128,128]{2,1,0:T(8,128)(2,1)} %get-tuple-element.87.key_value_grad_ref, f32[128,1536]{1,0:T(8,128)} %get-tuple-element.88.projected_ref, ...), custom_call_target="tpu_custom_call" | custom-call | tf_op jit(solution)/shard_map/project_back/pallas_call | solution.py:1282
  260.1 1.0 copy-done.3
  261.2 1.9 share.3
  263.1 2.1 bitcast_convert_fusion
  265.2 64.4 %reduce_weights.1 = (bf16[2,4,4,16,2304]{4,3,2,1,0:T(8,128)(2,1)}, bf16[2,4,4,16,2304]{4,3,2,1,0:T(8,128)(2,1)}, bf16[4,2,144,1024]{3,2,1,0:T(8,128)(2,1)}, bf16...) custom-call(bf16[2,4,4,16,2304]{4,3,2,1,0:T(8,128)(2,1)} %get-tuple-, ...), custom_call_target="tpu_custom_call", output_to_operand_aliasing={{0}: (0, {}), {1}: (1, {}), {2}: (2, {})} | custom-call | tf_op jit(solution)/shard_map/reduce_weights/pallas_call | solution.py:106
  329.5 1.3 fusion.17
  330.8 1.3 slice_bitcast_fusion
  332.1 10.2 %widen.1 = (f32[256,2048]{1,0:T(8,128)}, f32[256,1024]{1,0:T(8,128)}, f32[256,4608]{1,0:T(8,128)}, f32[256,4608]{1,0:T(8,128)}, f32[1152,1024]{1,0:T(8,128)}) custom-call(bf16[256,2048]{1,0:T(8,128)(2,1)} %bitcast.137, bf16[256,1024]{1,0:T(8,128)(2,1)} %bitcast.140, bf16[2,256,2304]{2,1,0:T(8,128)(2,1)} %bitcast.134, bf16[2,256,2304]{2,1,0:T(8,128)(2,1)} %bitcast.135, ...), custom_call_target="tpu_custom_call" | custom-call | tf_op jit(solution)/shard_map/widen/pallas_call | solution.py:643
  (44 shorter events, 6.6 us)
Async XLA Ops:
  48.6 1.0 copy-start.6
  49.5 0.9 copy-start.7
  71.1 1.0 copy-start
  72.1 0.7 copy-start.1
  72.8 41.4 %copy-start.9 = (bf16[2,2,4,4,16,1024]{5,4,3,2,1,0:T(8,128)(2,1)S(1)}, bf16[2,2,4,4,16,1024]{5,4,3,2,1,0:T(8,128)(2,1)}, u32[]{:S(2)}) copy-start(bf16[2,2,4,4,16,1024]{5,4,3,2,1,0:T(8,128)(2,1)} %get-tuple-element.69) | copy-start | bytes 6291460
  72.8 41.4 %copy-start.11 = (bf16[1,128,1024]{2,1,0:T(8,128)(2,1)S(1)}, bf16[1,128,1024]{2,1,0:T(8,128)(2,1)}, u32[]{:S(2)}) copy-start(bf16[1,128,1024]{2,1,0:T(8,128)(2,1)} %param.13) | copy-start | bytes 786436
  72.8 42.0 %copy-start.12 = (f32[1024]{0:T(1024)S(1)}, f32[1024]{0:T(1024)}, u32[]{:S(2)}) copy-start(f32[1024]{0:T(1024)} %param.23) | copy-start | bytes 12292
  72.8 42.1 %copy-start.8 = (bf16[128,1024]{1,0:T(8,128)(2,1)S(1)}, bf16[128,1024]{1,0:T(8,128)(2,1)}, u32[]{:S(2)}) copy-start(bf16[128,1024]{1,0:T(8,128)(2,1)} %get-tuple-element.70.refs_2_) | copy-start | bytes 786436
  106.3 8.6 %copy-start.2 = (bf16[1,128,1024]{2,1,0:T(8,128)(2,1)S(1)}, bf16[1,128,1024]{2,1,0:T(8,128)(2,1)}, u32[]{:S(2)}) copy-start(bf16[1,128,1024]{2,1,0:T(8,128)(2,1)} %param.14) | copy-start | bytes 786436
  106.3 1.0 copy-start.5
  114.2 3.3 copy-start.10
  114.9 4.0 %slice-start = ((s8[4718592]{0:T(1024)(128)(4,1)}), s8[4194304]{0:T(1024)(128)(4,1)S(1)}, s32[]{:S(2)}) async-start(s8[4718592]{0:T(1024)(128)(4,1)} %bitcast.117), calls=%async_computation | async-start | bytes 8388608
  117.5 1.4 slice-start.1
  117.5 2.8 slice-start.2
  118.9 1.4 slice-start.3
  140.3 5.1 %copy-start.4 = (bf16[8,128,128]{2,1,0:T(8,128)(2,1)}, bf16[8,128,128]{2,1,0:T(8,128)(2,1)S(1)}, u32[]{:S(2)}) copy-start(bf16[8,128,128]{2,1,0:T(8,128)(2,1)S(1)} %get-tuple-element.78) | copy-start | bytes 786436
  260.1 1.0 copy-start.3

commit v5 on v4

--- a/solution.py
+++ b/solution.py
@@ -621,7 +621,14 @@
     wires.finish_sends()
 
 
-def widen_kernel(qkv, out, gate, up, down, qkv_out, out_out, gate_out, up_out, down_out):
+def widen_kernel(
+    qkv, out, gate, up, down, gains, qkv_out, out_out, gate_out, up_out, down_out, attn_out,
+    ffn_out, query_out, key_out,
+):
+    attn_out[...] = gains[0:8, :]
+    ffn_out[...] = gains[8:16, :]
+    query_out[...] = gains[16:17, :HEAD_SIZE]
+    key_out[...] = gains[17:18, :HEAD_SIZE]
     qkv_out[...] = qkv[...].astype(F32)
     out_out[...] = out[...].astype(F32)
     down_out[...] = down[...].astype(F32)
@@ -633,11 +640,14 @@
                 whole[:, first : first + SLICE] = values.astype(F32)
 
 
-def widen(qkv, out, gate, up, down):
+def widen(qkv, out, gate, up, down, gains):
     steps = 8
 
     def rows(n, columns):
         return pl.BlockSpec((n // steps, columns), lambda i: (i, 0))
+
+    def whole(*dims):
+        return pl.BlockSpec(dims, lambda i: (0, 0))
 
     pair = pl.BlockSpec((2, 256 // steps, HALF_FF), lambda i: (0, i, 0))
     return pl.pallas_call(
@@ -649,14 +659,19 @@
             shape(256, FF, dtype=F32),
             shape(256, FF, dtype=F32),
             shape(SLICE, D, dtype=F32),
+            shape(8, 128, dtype=F32),
+            shape(8, 128, dtype=F32),
+            shape(1, HEAD_SIZE, dtype=F32),
+            shape(1, HEAD_SIZE, dtype=F32),
         ],
-        in_specs=[rows(256, 2048), rows(256, D), pair, pair, rows(SLICE, D)],
+        in_specs=[rows(256, 2048), rows(256, D), pair, pair, rows(SLICE, D), whole(24, 128)],
         out_specs=[
-            rows(256, 2048), rows(256, D), rows(256, FF), rows(256, FF), rows(SLICE, D)
+            rows(256, 2048), rows(256, D), rows(256, FF), rows(256, FF), rows(SLICE, D),
+            whole(8, 128), whole(8, 128), whole(1, HEAD_SIZE), whole(1, HEAD_SIZE),
         ],
         compiler_params=pltpu.CompilerParams(vmem_limit_bytes=60 * MIB),
         name="widen",
-    )(qkv, out, gate, up, down)
+    )(qkv, out, gate, up, down, gains)
 
 
 def reduce_weights(nears, qkv, out, gains):
@@ -687,14 +702,14 @@
         aliases={i: i for i in range(3)},
     )
 
-    widened = widen(
+    return widen(
         qkv.reshape(256, 2048),
         out.reshape(256, D),
         gate.reshape(2, 256, HALF_FF),
         up.reshape(2, 256, HALF_FF),
         down.reshape(SLICE, D),
-    )
-    return (*widened, gains)
+        gains,
+    )
 
 
 def head_columns(head):
@@ -1026,7 +1041,7 @@
         [pltpu.VMEM((SEQ, 128), BF16), pltpu.VMEM((1, SEQ), jnp.int32)],
         [SMEM] * 2 + [VMEM] * 2 + [HBM] * 3,
         [VMEM] * 3 + [HBM] * 3,
-        vmem=60 * MIB,
+        vmem=40 * MIB,
         aliases={4 + i: 3 + i for i in range(3)},
     )
     weights = (gate.reshape(D, HALF_FF), up.reshape(D, HALF_FF), down.reshape(HALF_FF, D))
@@ -1127,7 +1142,7 @@
     first_block = here.ctx // QUARTER * 16
     in_turn(
         [reduce(p) for p in range(3)]
-        + [attend_back_task((3, 3, 1, 1), first_block, *attention, *outs, *scratch)]
+        + [attend_back_task((3, 4, 1), first_block, *attention, *outs, *scratch)]
     )
     wires.finish_sends()
 
@@ -1179,15 +1194,12 @@
 
 
 def project_kernel(
-    x_ref, gain_ref, weight_hbm, query_gain_ref, key_gain_ref, cosine_ref, sine_ref, normed_ref,
-    query_ref, key_value_ref, projected_ref, weight_ref, weight_sem,
+    x_ref, gain_ref, weight_ref, query_gain_ref, key_gain_ref, cosine_ref, sine_ref, normed_ref,
+    query_ref, key_value_ref, projected_ref,
 ):
-    fetch = pltpu.make_async_copy(weight_hbm, weight_ref, weight_sem)
-    fetch.start()
     x = x_ref[...].astype(F32)
     normed = x * lax.rsqrt(jnp.mean(x * x, axis=-1, keepdims=True) + EPSILON) * gain_ref[...]
     normed_ref[...] = normed.astype(BF16)
-    fetch.wait()
     projected = nn(normed_ref[...], weight_ref[...])
     projected_ref[...] = projected[:, :1536]
     low = low_lanes()
@@ -1217,10 +1229,9 @@
             shape(TOKENS, D),
             shape(TOKENS, 1536, dtype=F32),
         ],
-        in_specs=[VMEM] * 2 + [ANY] + [VMEM] * 4,
+        in_specs=[VMEM] * 7,
         out_specs=[VMEM] * 4,
-        scratch_shapes=[pltpu.VMEM((D, 2048), BF16), pltpu.SemaphoreType.DMA],
-        compiler_params=pltpu.CompilerParams(vmem_limit_bytes=60 * MIB),
+        compiler_params=pltpu.CompilerParams(vmem_limit_bytes=32 * MIB),
         name="project",
     )(x, gain, weight, query_gain, key_gain, cosine, sine)
 
@@ -1421,25 +1432,20 @@
     )
 
     (projected_pair,) = share([grad_projected], [], 9)
-    grad_qkv, grad_out_weight, grad_gate_weight, grad_up_weight, grad_down, gains = reduce_weights(
+    *grads, attn_sum, ffn_sum, query_sum, key_sum = reduce_weights(
         nears,
         outer_sum(normed_half, projected_pair),
         outer_sum(attended_half, branch_pair.reshape(2 * TOKENS, D)),
         gains,
     )
-    gains = gains.reshape(-1)
     return (
         outputs.astype(BF16)[None],
         grad_inputs[None],
-        grad_qkv,
-        grad_out_weight,
-        grad_gate_weight,
-        grad_up_weight,
-        grad_down,
-        gains[:D],
-        gains[2 * D : 2 * D + HEAD_SIZE],
-        gains[2 * D + 128 : 2 * D + 128 + HEAD_SIZE],
-        gains[D : 2 * D],
+        *grads,
+        attn_sum.reshape(D),
+        query_sum.reshape(HEAD_SIZE),
+        key_sum.reshape(HEAD_SIZE),
+        ffn_sum.reshape(D),
     )
 
 

time: 343 us -> 336 us (0.980)
  Pallas kernels: 303 us -> 298 us
    pallas_call x1, Pallas kernels: 5.97 us -> 2.14 us  [project(): pl.pallas_call(project_kernel, out_shape=[shape(TOKENS, D), shape(TOKENS,...]
    unnamed x34 -> x46, local copies, waits for them, and re-layouts: 5.64 us -> 6.96 us
where the time goes in v5:
time: 336 us; the launch traced here: 335 us
  Pallas kernels  298 us (89%)
  matrix products  25.2 us (8%)
  local copies, waits for them, and re-layouts  6.96 us (2%)
  other arithmetic  3.9 us (1%)
    pallas_call x11, Pallas kernels, wired_call(): pl.pallas_call(kernel, out_shape=outs, in_specs=[ANY] * len(ins) if in_sp...  278 us
    dot_general x5, matrix products, outer_sum(): lax.dot_general(left, right, (((0,), (0,)), ((), ())), preferred_element_...  14.4 us
    dot_general x8, matrix products, matmul(): return jnp.dot(left, right, preferred_element_type=F32)  10.8 us
    pallas_call x1, Pallas kernels, widen(): pl.pallas_call(widen_kernel, grid=(steps,), out_shape=[shape(256, 2048, d...  10.3 us
    unnamed x46, local copies, waits for them, and re-layouts  6.96 us
    pallas_call x1, Pallas kernels, project_back(): pl.pallas_call(project_back_kernel, out_shape=[shape(TOKENS, 2048), shape...  6.87 us

profile of v5, /device:TPU:0, one launch (start us, length us, event | category | flops | bytes accessed | tf_op | source)
XLA Modules:
  0.0 334.9 jit_solution(4587302759430467554)
XLA Ops:
  1.4 0.8 maximum_bitcast_fusion
  2.6 39.0 %gather.1 = (bf16[2,2,4,4,16,2048]{5,4,3,2,1,0:T(8,128)(2,1)}, bf16[2,2,4,4,16,1024]{5,4,3,2,1,0:T(8,128)(2,1)}, bf16[2,2,4,4,16,2304]{5,4,3,2,1,0:T(8,128)(2,1)...) custom-call(bf16[4,4,16,2048]{3,2,1,0:T(8,128)(2,1)} %bitcast.137, ...), custom_call_target="tpu_custom_call" | custom-call | tf_op jit(solution)/shard_map/gather/pallas_call | solution.py:106
  41.7 2.2 copy-done
  43.9 2.1 project.1
  46.1 0.9 copy-done.8
  47.0 20.6 %to_heads.1 = (bf16[8,128,128]{2,1,0:T(8,128)(2,1)S(1)}, bf16[32,128,128]{2,1,0:T(8,128)(2,1)S(1)}) custom-call(bf16[128,1024]{1,0:T(8,128)(2,1)S(1)} %get-tuple-element.65.query, bf16[128,1024]{1,0:T(8,128)(2,1)S(1)} %get-tuple-element.66.key_value), custom_call_target="tpu_custom_call" | custom-call | tf_op jit(solution)/shard_map/to_heads/pallas_call | solution.py:106
  67.6 2.8 copy-done.2
  70.4 30.6 %attend.1 = (bf16[16,64,128]{2,1,0:T(8,128)(2,1)S(1)}, f32[16,128,128]{2,1,0:T(8,128)S(1)}, f32[16,8,128]{2,1,0:T(8,128)S(1)}, bf16[2,2,4,4,16,2304]{5,4,3,2,1,0...) custom-call(s32[4]{0:T(128)S(1)} %bitcast.118, ...), custom_call_target="tpu_custom_call", output_to_operand_aliasing={{3}: (4, {}), {4}: (5, {}), {5}: (6, {})} | custom-call | tf_op jit(solution)/shard_map/attend/pallas_call | solution.py:106
  101.1 7.0 %to_tokens.1.refs_3_ = bf16[128,1024]{1,0:T(8,128)(2,1)S(1)} custom-call(bf16[8,128,128]{2,1,0:T(8,128)(2,1)S(1)} %bitcast.114), custom_call_target="tpu_custom_call" | custom-call | tf_op jit(solution)/shard_map/to_tokens/pallas_call | solution.py:106
  108.8 2.6 share.2
  111.4 1.4 fusion.18
  112.8 1.4 fusion.17
  114.2 2.4 multiply_convert_fusion
  116.7 1.4 fusion.20
  118.1 1.4 convolution_add_fusion
  119.5 1.4 fusion.19.refs_0_
  120.9 2.8 hand_over.1
  124.5 1.1 fusion.15
  125.6 0.8 convolution_convert_fusion.3.grad
  126.4 7.7 %grad_to_heads.1 = (bf16[8,128,128]{2,1,0:T(8,128)(2,1)S(1)}, bf16[2,128,1024]{2,1,0:T(8,128)(2,1)S(1)}) custom-call(bf16[128,1024]{1,0:T(8,128)(2,1)S(1)} %convolution_convert_fusion.3.grad, bf16[128,1024]{1,0:T(8,128)(2,1)S(1)} %get-tuple-element.119.branch), custom_call_target="tpu_custom_call" | custom-call | tf_op jit(solution)/shard_map/grad_to_heads/pallas_call | solution.py:106
  134.1 1.5 bitcast_convert_fusion.1
  135.6 3.6 %convolution_convert_fusion.1 = bf16[1024,2304]{1,0:T(8,128)(2,1)} fusion(bf16[256,1024]{1,0:T(8,128)(2,1)S(1)} %bitcast.96, bf16[256,2304]{1,0:T(8,128)(2,1)S(1)} %get-tuple-element.122), kind=kOutput, calls=%fused_computation.1 | convolution fusion | flops 1210318848 | bytes 6422528 | tf_op jit(solution)/shard_map/dot_general | solution.py:1319
  139.3 3.6 %convolution_convert_fusion.2 = bf16[1024,2304]{1,0:T(8,128)(2,1)} fusion(bf16[256,1024]{1,0:T(8,128)(2,1)S(1)} %bitcast.97, bf16[256,2304]{1,0:T(8,128)(2,1)S(1)} %get-tuple-element.123), kind=kOutput, calls=%fused_computation.2 | convolution fusion | flops 1210318848 | bytes 6422528 | tf_op jit(solution)/shard_map/dot_general | solution.py:1319
  142.9 3.6 %convolution_convert_fusion = bf16[2304,1024]{1,0:T(8,128)(2,1)} fusion(bf16[256,2304]{1,0:T(8,128)(2,1)S(1)} %get-tuple-element.124, bf16[256,1024]{1,0:T(8,128)(2,1)S(1)} %bitcast.112), kind=kOutput, calls=%fused_computation | convolution fusion | flops 1210318848 | bytes 6422528 | tf_op jit(solution)/shard_map/dot_general | solution.py:1319
  146.5 68.2 %attend_back.1 = (bf16[16,64,128]{2,1,0:T(8,128)(2,1)}, bf16[4096,128]{1,0:T(8,128)(2,1)}, bf16[2,4,4,16,2304]{4,3,2,1,0:T(8,128)(2,1)}, bf16[2,4,4,16,2304]{4,3,2,1,0:T(8,128)(2,1)}, bf16[4,2,144,1024]{3,2,1,0:T(8,128)(2,1)}) custom-call(s32[4]{0:T(128)} %bitcast.117, s32[64]{0:T(128)} %refs_1_.1, bf16[16,64,128]{2,1,0:T(8,128)(2,1)} %bitcast.109, ...), custom_call_target="tpu_custom_call" | custom-call | tf_op jit(solution)/shard_map/attend_back/pallas_call | solution.py:106
  214.7 33.2 %grads_to_tokens.1 = (bf16[128,1024]{1,0:T(8,128)(2,1)}, bf16[32,128,128]{2,1,0:T(8,128)(2,1)}, bf16[2,4,4,16,2304]{4,3,2,1,0:T(8,128)(2,1)}, bf16[2,4,4,16,2304...) custom-call(bf16[8,128,128]{2,1,0:T(8,128)(2,1)} %bitcast.142, ...), custom_call_target="tpu_custom_call", output_to_operand_aliasing={{2}: (2, {}), {3}: (3, {}), {4}: (4, {})} | custom-call | tf_op jit(solution)/shard_map/grads_to_tokens/pallas_call | solution.py:106
  247.9 6.9 %project_back.1 = (bf16[128,2048]{1,0:T(8,128)(2,1)}, bf16[128,1024]{1,0:T(8,128)(2,1)}, f32[24,128]{1,0:T(8,128)}) custom-call(bf16[128,1024]{1,0:T(8,128)(2,1)} %get-tuple-element.90.query_grad_ref, bf16[32,128,128]{2,1,0:T(8,128)(2,1)} %get-tuple-element.91.key_value_grad_ref, f32[128,1536]{1,0:T(8,128)} %copy-done.8, bf16[128,1024]{1,0:T(8,128)(2,1)} %bitcast.106, ...), custom_call_target="tpu_custom_call" | custom-call | tf_op jit(solution)/shard_map/project_back/pallas_call | solution.py:1293
  254.8 1.0 copy-done.11
  255.8 1.9 share.3
  257.8 2.1 bitcast_convert_fusion
  259.8 64.6 %reduce_weights.1 = (bf16[2,4,4,16,2304]{4,3,2,1,0:T(8,128)(2,1)}, bf16[2,4,4,16,2304]{4,3,2,1,0:T(8,128)(2,1)}, bf16[4,2,144,1024]{3,2,1,0:T(8,128)(2,1)}, bf16...) custom-call(bf16[2,4,4,16,2304]{4,3,2,1,0:T(8,128)(2,1)} %get-tuple-, ...), custom_call_target="tpu_custom_call", output_to_operand_aliasing={{0}: (0, {}), {1}: (1, {}), {2}: (2, {})} | custom-call | tf_op jit(solution)/shard_map/reduce_weights/pallas_call | solution.py:106
  324.4 10.3 %widen.1 = (f32[256,2048]{1,0:T(8,128)}, f32[256,1024]{1,0:T(8,128)}, f32[256,4608]{1,0:T(8,128)}, f32[256,4608]{1,0:T(8,128)}, f32[1152,1024]{1,0:T(8,128)}, /*...) custom-call(bf16[256,2048]{1,0:T(8,128)(2,1)} %bitcast.138, ...), custom_call_target="tpu_custom_call" | custom-call | tf_op jit(solution)/shard_map/widen/pallas_call | solution.py:653
  (53 shorter events, 2.6 us)
Async XLA Ops:
  2.2 39.4 %copy-start.15 = (f32[1,128]{1,0:T(1,128)}, f32[1,128]{1,0:T(1,128)S(1)}, u32[]{:S(2)}) copy-start(f32[1,128]{1,0:T(1,128)S(1)} %get-tuple-element.132.query_gain_ref) | copy-start | bytes 1540
  2.3 39.4 %copy-start.16 = (f32[1,128]{1,0:T(1,128)}, f32[1,128]{1,0:T(1,128)S(1)}, u32[]{:S(2)}) copy-start(f32[1,128]{1,0:T(1,128)S(1)} %get-tuple-element.133.key_gain_ref) | copy-start | bytes 1540
  2.6 39.1 %copy-start.9 = (f32[128,128]{1,0:T(8,128)}, f32[128,128]{1,0:T(8,128)S(1)}, u32[]{:S(2)}) copy-start(f32[128,128]{1,0:T(8,128)S(1)} %get-tuple-element.126.sine_ref) | copy-start | bytes 196612
  2.6 39.1 %copy-start.10 = (f32[128,128]{1,0:T(8,128)}, f32[128,128]{1,0:T(8,128)S(1)}, u32[]{:S(2)}) copy-start(f32[128,128]{1,0:T(8,128)S(1)} %get-tuple-element.127.cosine_ref) | copy-start | bytes 196612
  2.6 39.1 %copy-start.4 = (bf16[1,128,1024]{2,1,0:T(8,128)(2,1)S(1)}, bf16[1,128,1024]{2,1,0:T(8,128)(2,1)}, u32[]{:S(2)}) copy-start(bf16[1,128,1024]{2,1,0:T(8,128)(2,1)} %param.13) | copy-start | bytes 786436
  2.6 39.1 %copy-start.14 = (f32[1024]{0:T(1024)S(1)}, f32[1024]{0:T(1024)}, u32[]{:S(2)}) copy-start(f32[1024]{0:T(1024)} %param.20) | copy-start | bytes 12292
  41.7 2.2 copy-start
  43.9 23.7 %copy-start.1 = (bf16[2,2,4,4,16,2304]{5,4,3,2,1,0:T(8,128)(2,1)S(1)}, bf16[2,2,4,4,16,2304]{5,4,3,2,1,0:T(8,128)(2,1)}, u32[]{:S(2)}) copy-start(bf16[2,2,4,4,16,2304]{5,4,3,2,1,0:T(8,128)(2,1)} %get-tuple-element.69.gate_in) | copy-start | bytes 14155780
  43.9 23.7 %copy-start.17 = (s32[1,4]{1,0:T(1,128)S(1)}, s32[1,4]{1,0:T(1,128)}, u32[]{:S(2)}) copy-start(s32[1,4]{1,0:T(1,128)} %param.25) | copy-start | bytes 52
  43.9 23.7 %copy-start.18 = (s32[64]{0:T(128)S(1)}, s32[64]{0:T(128)}, u32[]{:S(2)}) copy-start(s32[64]{0:T(128)} %refs_1_.1) | copy-start | bytes 772
  46.1 0.9 copy-start.8
  67.5 33.5 %copy-start.3 = (bf16[32,128,128]{2,1,0:T(8,128)(2,1)}, bf16[32,128,128]{2,1,0:T(8,128)(2,1)S(1)}, u32[]{:S(2)}) copy-start(bf16[32,128,128]{2,1,0:T(8,128)(2,1)S(1)} %get-tuple-element.68) | copy-start | bytes 3145732
  67.6 33.5 %copy-start.5 = (bf16[8,128,128]{2,1,0:T(8,128)(2,1)}, bf16[8,128,128]{2,1,0:T(8,128)(2,1)S(1)}, u32[]{:S(2)}) copy-start(bf16[8,128,128]{2,1,0:T(8,128)(2,1)S(1)} %get-tuple-element.67) | copy-start | bytes 786436
  67.6 2.8 copy-start.2
  70.4 37.7 %copy-start.19 = (bf16[2,2,4,4,16,1024]{5,4,3,2,1,0:T(8,128)(2,1)S(1)}, bf16[2,2,4,4,16,1024]{5,4,3,2,1,0:T(8,128)(2,1)}, u32[]{:S(2)}) copy-start(bf16[2,2,4,4,16,1024]{5,4,3,2,1,0:T(8,128)(2,1)} %get-tuple-element.73) | copy-start | bytes 6291460
  101.0 7.7 %copy-start.13 = (f32[16,8,128]{2,1,0:T(8,128)}, f32[16,8,128]{2,1,0:T(8,128)S(1)}, u32[]{:S(2)}) copy-start(f32[16,8,128]{2,1,0:T(8,128)S(1)} %get-tuple-element.84.refs_6_) | copy-start | bytes 196612
  101.0 10.4 %copy-start.6 = (f32[16,128,128]{2,1,0:T(8,128)}, f32[16,128,128]{2,1,0:T(8,128)S(1)}, u32[]{:S(2)}) copy-start(f32[16,128,128]{2,1,0:T(8,128)S(1)} %get-tuple-element.83.refs_5_) | copy-start | bytes 3145732
  101.0 7.6 %copy-start.20 = (f32[1024]{0:T(1024)S(1)}, f32[1024]{0:T(1024)}, u32[]{:S(2)}) copy-start(f32[1024]{0:T(1024)} %param.23) | copy-start | bytes 12292
  101.1 7.8 %copy-start.7 = (bf16[1,128,1024]{2,1,0:T(8,128)(2,1)S(1)}, bf16[1,128,1024]{2,1,0:T(8,128)(2,1)}, u32[]{:S(2)}) copy-start(bf16[1,128,1024]{2,1,0:T(8,128)(2,1)} %param.14) | copy-start | bytes 786436
  111.4 2.8 slice-start
  112.8 1.4 slice-start.1
  134.1 5.1 %copy-start.12 = (bf16[8,128,128]{2,1,0:T(8,128)(2,1)}, bf16[8,128,128]{2,1,0:T(8,128)(2,1)S(1)}, u32[]{:S(2)}) copy-start(bf16[8,128,128]{2,1,0:T(8,128)(2,1)S(1)} %get-tuple-element.82) | copy-start | bytes 786436
  254.8 1.0 copy-start.11
